TPU v7x, 32 devices: a whole 2x2x4 slice. The times are simulated.
32 devices in a mesh: grp: 2 (over x), par: 16 (over z, y, core).
Axes of the slice: x: 2, y: 2, z: 4, core: 2. Of those that a mesh axis runs over, the one named last changes fastest.
Arguments:
- omega: bfloat16 [32, 131072], P(None, 'par'), may hold values from -6 to 6
- jac_blocks: bfloat16 [2, 2048, 128, 128], P('grp', 'par'), may hold values from -0.1796875 to 0.1796875
- block_param: int32 [2, 2048], P('grp', 'par'), may hold values from 0 to 63
- block_obs: int32 [2, 2048], P('grp', 'par'), may hold values from 0 to 63
- block_count: int32 [2, 16], P('grp', 'par'), may hold values from 16 to 128, as said below
- obs_weight: float32 [2, 8192], P('grp'), may hold values from 0.1 to 1
Outputs:
- hess_probe: float32 [32, 131072], P(None, ('par', 'grp'))
Inputs may be any that keep to these rules, and one draw needn't show every extreme that they name: `block_count`: in every group four devices use all 128 slots and one device uses the fewest; the others use at most 64.
All inputs are finite; a program needn't handle non-finite values.
Results may differ from a plain program's by a relative error of at most 0.0027.
Values may be sent and summed in bfloat16 or wider, within the bound.
A program may use at most 64 MiB of HBM per device.

v0:
```python
import jax
import jax.numpy as jnp
from jax import lax
from jax.sharding import PartitionSpec as P


def on_device(omega, jac_blocks, block_param, block_obs, block_count, obs_weight):
    probes = omega.shape[0]
    width = jac_blocks.shape[2]
    slots = jac_blocks.shape[1]
    pblocks = omega.shape[1] // width
    oblocks = obs_weight.shape[1] // width
    blocks = jac_blocks[0]
    bparam = block_param[0]
    bobs = block_obs[0]
    weights = obs_weight[0]
    active = (jnp.arange(slots, dtype=jnp.int32) < block_count[0, 0]).astype(jnp.float32)
    panels = omega.reshape(probes, pblocks, width)
    picked = jnp.take(panels, bparam, axis=1)
    terms = jnp.einsum("kcp,cpo->cko", picked, blocks, preferred_element_type=jnp.float32)
    terms = terms * active[:, None, None]
    partial_value = jax.ops.segment_sum(terms, bobs, num_segments=oblocks)
    partial_value = jnp.transpose(partial_value, (1, 0, 2)).reshape(probes, oblocks * width)
    fwd = lax.psum(partial_value, "par")
    scaled = (fwd * weights[None, :]).astype(jnp.bfloat16)
    vblocks = scaled.reshape(probes, oblocks, width)
    pickv = jnp.take(vblocks, bobs, axis=1)
    back = jnp.einsum("kco,cpo->ckp", pickv, blocks, preferred_element_type=jnp.float32)
    back = back * active[:, None, None]
    local_terms = jax.ops.segment_sum(back, bparam, num_segments=pblocks)
    local_terms = jnp.transpose(local_terms, (1, 0, 2)).reshape(probes, pblocks * width)
    return lax.psum_scatter(local_terms, "grp", scatter_dimension=1, tiled=True)


def solution(mesh):
    in_specs = (
        P(None, "par"),
        P("grp", "par", None, None),
        P("grp", "par"),
        P("grp", "par"),
        P("grp", "par"),
        P("grp", None),
    )
    out_specs = P(None, ("par", "grp"))
    return jax.shard_map(
        on_device, mesh=mesh, in_specs=in_specs, out_specs=out_specs, check_vma=False
    )
```

profile of v0, /device:TPU:0, one launch (start us, length us, event | category | flops | bytes accessed | tf_op | source)
XLA Modules:
  0.0 170.8 jit_solution(9352120180000015508)
XLA Ops:
  6.5 0.0 copy-start
  6.5 0.0 all-reduce.2.cloned.1.call-start
  7.2 0.7 compare_select_fusion.1
  7.9 0.7 compare_and_fusion.1
  8.6 0.1 copy_bitcast_fusion.3
  8.7 0.8 gather_fusion
  9.4 0.0 copy-start.3
  9.5 4.8 %fusion.4 = f32[128,32,128]{2,1,0:T(8,128)} fusion(bf16[1,128,128,128]{3,2,1,0:T(8,128)(2,1)} %param.9, bf16[128,32,128]{2,1,0:T(8,128)(2,1)S(1)} %gather_fusion, f32[128]{0:T(128)S(1)} %get-tuple-element.7, pred[128]{0:T(512)(128)(4,1)S(1)} %get-tuple-element.6), kind=kOutput, calls=%fused_computation.8 | convolution fusion | flops 135266304 | bytes 7340672 | tf_op jit(solution)/shard_map/kcp,cpo->cko/dot_general | solution.py:20
  14.3 0.1 broadcast.10.clone
  14.4 11.7 %scatter_fusion = f32[64,32,128]{2,1,0:T(8,128)S(1)} fusion(f32[64,32,128]{2,1,0:T(8,128)S(1)} %broadcast.10.clone, s32[128]{0:T(128)S(1)} %bitcast.50, f32[128,32,128]{2,1,0:T(8,128)} %fusion.4), kind=kCustom, calls=%fused_computation.2 | custom fusion | flops 524288 | bytes 6291968 | tf_op jit(solution)/shard_map/scatter-add | solution.py:22
  26.1 0.0 copy-start.1
  26.1 1.1 copy_bitcast_fusion.1
  27.2 0.0 all-reduce.2.cloned.1.call-update
  27.2 0.0 reduce-scatter.2.cloned.1.call-start
  27.3 96.0 %all-reduce.2.cloned.1.call-done = f32[32,8192]{1,0:T(8,128)} async-done(((f32[32,8192]{1,0:T(8,128)}), f32[32,8192]{1,0:T(8,128)}) %all-reduce.2.cloned.1.call-update) | async-done | bytes 1048592 | tf_op jit(solution)/shard_map/psum | solution.py:24
  123.3 1.3 copy_bitcast_fusion.2
  124.7 0.8 gather_fusion.1
  125.4 0.0 copy-start.2
  125.4 5.9 %fusion.7 = f32[128,32,128]{2,1,0:T(8,128)} fusion(bf16[1,128,128,128]{3,2,1,0:T(8,128)(2,1)} %param.9, bf16[128,32,128]{2,1,0:T(8,128)(2,1)S(1)} %gather_fusion.1, f32[128]{0:T(128)S(1)} %get-tuple-element.7, pred[128]{0:T(512)(128)(4,1)S(1)} %compare_and_fusion), kind=kOutput, calls=%fused_computation.9 | convolution fusion | flops 135266304 | bytes 7340672 | tf_op jit(solution)/shard_map/kco,cpo->ckp/dot_general | solution.py:28
  131.3 0.1 broadcast.10
  131.4 11.7 %scatter_fusion.1 = f32[64,32,128]{2,1,0:T(8,128)S(1)} fusion(f32[64,32,128]{2,1,0:T(8,128)S(1)} %broadcast.10, s32[128]{0:T(128)S(1)} %bitcast.49, f32[128,32,128]{2,1,0:T(8,128)} %fusion.7), kind=kCustom, calls=%fused_computation.3 | custom fusion | flops 524288 | bytes 6291968 | tf_op jit(solution)/shard_map/scatter-add | solution.py:30
  143.2 1.1 copy_bitcast_fusion
  144.2 0.0 reduce-scatter.2.cloned.1.call-update
  144.2 19.7 %reduce-scatter.2.cloned.1.call-done = f32[32,4096]{1,0:T(8,128)} async-done(((f32[32,8192]{1,0:T(8,128)}), f32[32,4096]{1,0:T(8,128)}) %reduce-scatter.2.cloned.1.call-update) | async-done | bytes 524304 | tf_op jit(solution)/shard_map/reduce_scatter | solution.py:32
  (8 shorter events, 0.0 us)
Async XLA Ops:
  6.5 2.0 %copy-start = (bf16[32,8192]{1,0:T(8,128)(2,1)S(1)}, bf16[32,8192]{1,0:T(8,128)(2,1)}, u32[]{:S(2)}) copy-start(bf16[32,8192]{1,0:T(8,128)(2,1)} %param.8) | copy-start | bytes 1572868
  6.5 116.8 %all-reduce.2.cloned.1.call-start = ((), (), s32[]{:S(2)}) async-start(), calls=%async_computation.1 | async-start | bytes 2097152 | tf_op jit(solution)/shard_map/psum | solution.py:24
  9.4 4.9 %copy-start.3 = (s32[1,128]{1,0:T(1,128)S(1)}, s32[1,128]{1,0:T(1,128)}, u32[]{:S(2)}) copy-start(s32[1,128]{1,0:T(1,128)} %param.11) | copy-start | bytes 1540
  26.1 97.2 %copy-start.1 = (f32[1,8192]{1,0:T(1,128)S(1)}, f32[1,8192]{1,0:T(1,128)}, u32[]{:S(2)}) copy-start(f32[1,8192]{1,0:T(1,128)} %param.13) | copy-start | bytes 98308
  27.2 136.7 %reduce-scatter.2.cloned.1.call-start = ((), (), s32[]{:S(2)}) async-start(), calls=%async_computation.2 | async-start | bytes 1572864 | tf_op jit(solution)/shard_map/reduce_scatter | solution.py:32
  125.4 6.0 %copy-start.2 = (s32[1,128]{1,0:T(1,128)S(1)}, s32[1,128]{1,0:T(1,128)}, u32[]{:S(2)}) copy-start(s32[1,128]{1,0:T(1,128)} %param.10) | copy-start | bytes 1540
Sparse Core Ops, SparseCore 0:
  27.4 95.9 all-reduce.1
  144.4 19.5 reduce-scatter.1
where the time goes:
time: 171 us
  waiting for transfers between devices  116 us (68%)
  other arithmetic  26.1 us (15%)
  between operations  14.2 us (8%)
  matrix products  10.7 us (6%)
  local copies, waits for them, and re-layouts  4.02 us (2%)
    psum x1, waiting for transfers between devices, on_device(): fwd = lax.psum(partial_value, 'par')  96 us
    reduce_scatter x1, waiting for transfers between devices, on_device(): return lax.psum_scatter(local_terms, 'grp', scatter_dimension=1, tiled=True)  19.7 us
    scatter-add x1, other arithmetic, on_device(): local_terms = jax.ops.segment_sum(back, bparam, num_segments=pblocks)  11.7 us
    scatter-add x1, other arithmetic, on_device(): partial_value = jax.ops.segment_sum(terms, bobs, num_segments=oblocks)  11.7 us
    dot_general x1, matrix products, on_device(): jnp.einsum('kco,cpo->ckp', pickv, blocks, preferred_element_type=jnp.floa...  5.88 us
    dot_general x1, matrix products, on_device(): jnp.einsum('kcp,cpo->cko', picked, blocks, preferred_element_type=jnp.flo...  4.81 us
  transfers between devices with their start and end apart: 2, of which 2 were waited for; matrix products, arithmetic and copies ran while one was open for 0% of the time, Pallas kernels for 0%

commit v1 on v0

v1 whole, which is shorter than its diff:
```python
import functools

import jax
import jax.numpy as jnp
from jax import lax
from jax.experimental import pallas as pl
from jax.experimental.pallas import tpu as pltpu
from jax.sharding import PartitionSpec as P

MESH = pl.DeviceIdType.MESH
STEP = 32
WIRE = jnp.float32


def fwd_kernel(bparam, bobs, count, omega_ref, blocks_ref, out_ref, acc):
    i = pl.program_id(0)
    oblocks = out_ref.shape[0]
    width = blocks_ref.shape[2]

    @pl.when(i == 0)
    def _():
        acc[...] = jnp.zeros_like(acc)

    for j in range(blocks_ref.shape[0]):
        s = i * blocks_ref.shape[0] + j
        to = jnp.where(s < count[0, 0], bobs[0, s], oblocks)
        at = pl.multiple_of(bparam[0, s] * width, width)
        acc[to] += jnp.dot(
            omega_ref[:, pl.ds(at, width)], blocks_ref[j], preferred_element_type=jnp.float32
        )

    @pl.when(i == pl.num_programs(0) - 1)
    def _():
        out_ref[...] = acc[0:oblocks]


def back_kernel(bparam, bobs, count, scaled_ref, blocks_ref, out_ref, acc):
    i = pl.program_id(0)
    pblocks = out_ref.shape[0]

    @pl.when(i == 0)
    def _():
        acc[...] = jnp.zeros_like(acc)

    for j in range(blocks_ref.shape[0]):
        s = i * blocks_ref.shape[0] + j
        to = jnp.where(s < count[0, 0], bparam[0, s], pblocks)
        acc[to] += lax.dot_general(
            scaled_ref[bobs[0, s]],
            blocks_ref[j],
            (((1,), (1,)), ((), ())),
            preferred_element_type=jnp.float32,
        )

    @pl.when(i == pl.num_programs(0) - 1)
    def _():
        out_ref[...] = acc[0:pblocks]


def sparse_call(kernel, bparam, bobs, count, dense, blocks, outs, probes):
    slots, width = blocks.shape[1], blocks.shape[2]
    whole = tuple(0 for _ in dense.shape)
    return pl.pallas_call(
        kernel,
        out_shape=jax.ShapeDtypeStruct((outs, probes, width), jnp.float32),
        grid_spec=pltpu.PrefetchScalarGridSpec(
            num_scalar_prefetch=3,
            grid=(slots // STEP,),
            in_specs=[
                pl.BlockSpec(dense.shape, lambda i, *_: whole),
                pl.BlockSpec((None, STEP, width, width), lambda i, *_: (0, i, 0, 0)),
            ],
            out_specs=pl.BlockSpec((outs, probes, width), lambda i, *_: (0, 0, 0)),
            scratch_shapes=[pltpu.VMEM((outs + 1, probes, width), jnp.float32)],
        ),
        compiler_params=pltpu.CompilerParams(vmem_limit_bytes=32 * 1024 * 1024),
        cost_estimate=pl.CostEstimate(
            flops=2 * slots * probes * width * width,
            bytes_accessed=2 * slots * width * width,
            transcendentals=0,
        ),
    )(bparam, bobs, count, dense, blocks)


def reduce_kernel(
    n, part_ref, weight_ref, out_ref, sib, sbuf, rbuf,
    s1, r1, s2, r2, s3, r3, s4, r4,
):
    me = lax.axis_index("par")
    chips = n // 2
    q, c = me // 2, lax.rem(me, 2)
    oblocks, _, width = part_ref.shape
    half = oblocks // 2
    nb = half // chips
    mate = {"par": 2 * q + 1 - c}

    def chip(i):
        return lax.rem(q + i, chips)

    def peer(t):
        return {"par": 2 * t + c}

    def mine(t):
        return pl.ds(c * half + t * nb, nb)

    def theirs(t):
        return pl.ds((1 - c) * half + t * nb, nb)

    barrier = pltpu.get_barrier_semaphore()
    pl.semaphore_signal(barrier, inc=1, device_id=mate, device_id_type=MESH)
    for i in range(1, chips):
        pl.semaphore_signal(barrier, inc=1, device_id=peer(chip(i)), device_id_type=MESH)
    pl.semaphore_wait(barrier, chips)

    def to_mate(t):
        return pltpu.make_async_remote_copy(
            src_ref=part_ref.at[theirs(t)], dst_ref=sib.at[t],
            send_sem=s1.at[t], recv_sem=r1.at[t], device_id=mate, device_id_type=MESH)

    def to_owner(t):
        return pltpu.make_async_remote_copy(
            src_ref=sbuf.at[t], dst_ref=rbuf.at[q],
            send_sem=s2.at[t], recv_sem=r2.at[q], device_id=peer(t), device_id_type=MESH)

    def from_chip(t):
        return pltpu.make_async_remote_copy(
            src_ref=sbuf.at[t], dst_ref=rbuf.at[t],
            send_sem=s2.at[t], recv_sem=r2.at[t], device_id=peer(t), device_id_type=MESH)

    def gather_to(t):
        return pltpu.make_async_remote_copy(
            src_ref=out_ref.at[mine(q)], dst_ref=out_ref.at[mine(q)],
            send_sem=s3.at[t], recv_sem=r3.at[q], device_id=peer(t), device_id_type=MESH)

    def gather_from(t):
        return pltpu.make_async_remote_copy(
            src_ref=out_ref.at[mine(t)], dst_ref=out_ref.at[mine(t)],
            send_sem=s3.at[t], recv_sem=r3.at[t], device_id=peer(t), device_id_type=MESH)

    def hand_over(t):
        return pltpu.make_async_remote_copy(
            src_ref=out_ref.at[mine(t)], dst_ref=out_ref.at[mine(t)],
            send_sem=s4.at[t], recv_sem=r4.at[t], device_id=mate, device_id_type=MESH)

    def take_over(t):
        return pltpu.make_async_remote_copy(
            src_ref=out_ref.at[theirs(t)], dst_ref=out_ref.at[theirs(t)],
            send_sem=s4.at[t], recv_sem=r4.at[t], device_id=mate, device_id_type=MESH)

    for i in range(1, chips + 1):
        to_mate(chip(i)).start()
    for i in range(1, chips):
        t = chip(i)
        to_mate(t).wait_recv()
        sbuf[t] = (part_ref[mine(t)] + sib[t]).astype(sbuf.dtype)
        to_owner(t).start()
    to_mate(q).wait_recv()
    total = part_ref[mine(q)] + sib[q]
    for i in range(1, chips):
        t = chip(chips - i)
        from_chip(t).wait_recv()
        total += rbuf[t].astype(jnp.float32)
    for b in range(nb):
        block = c * half + q * nb + b
        weight = weight_ref[0:1, pl.ds(pl.multiple_of(block * width, width), width)]
        out_ref[block] = (total[b] * weight).astype(out_ref.dtype)
    for i in range(1, chips):
        gather_to(chip(i)).start()
    hand_over(q).start()
    for i in range(1, chips):
        t = chip(chips - i)
        gather_from(t).wait_recv()
        hand_over(t).start()
    for i in range(chips):
        take_over(chip(i)).wait_recv()
    for i in range(chips):
        t = chip(i)
        to_mate(t).wait_send()
        hand_over(t).wait_send()
    for i in range(1, chips):
        t = chip(i)
        to_owner(t).wait_send()
        gather_to(t).wait_send()


def reduce_call(n, part, weights):
    oblocks, probes, width = part.shape
    chips = n // 2
    nb = oblocks // n
    dma = pltpu.SemaphoreType.DMA((chips,))
    vmem = pl.BlockSpec(memory_space=pltpu.VMEM)
    return pl.pallas_call(
        functools.partial(reduce_kernel, n),
        out_shape=jax.ShapeDtypeStruct(part.shape, jnp.bfloat16),
        in_specs=[vmem, vmem],
        out_specs=vmem,
        scratch_shapes=[
            pltpu.VMEM((chips, nb, probes, width), jnp.float32),
            pltpu.VMEM((chips, nb, probes, width), WIRE),
            pltpu.VMEM((chips, nb, probes, width), WIRE),
        ] + [dma] * 8,
        compiler_params=pltpu.CompilerParams(
            collective_id=0, has_side_effects=True, vmem_limit_bytes=32 * 1024 * 1024),
        cost_estimate=pl.CostEstimate(flops=0, bytes_accessed=4 * part.size, transcendentals=0),
    )(part, weights)


def exchange_kernel(groups, chunks, back_ref, out_ref, sbuf, rbuf, ss, rs):
    g = lax.axis_index("grp")
    pblocks, probes, width = back_ref.shape
    per = pblocks // groups
    cb = per // chunks

    def other(i):
        return lax.rem(g + i, groups)

    def copy(t, lands, k):
        return pltpu.make_async_remote_copy(
            src_ref=sbuf.at[t, pl.ds(k * cb, cb)], dst_ref=rbuf.at[lands, pl.ds(k * cb, cb)],
            send_sem=ss.at[t, k], recv_sem=rs.at[lands, k],
            device_id={"grp": t}, device_id_type=MESH)

    barrier = pltpu.get_barrier_semaphore()
    for i in range(1, groups):
        pl.semaphore_signal(barrier, inc=1, device_id={"grp": other(i)}, device_id_type=MESH)
    pl.semaphore_wait(barrier, groups - 1)

    for k in range(chunks):
        for i in range(1, groups):
            t = other(i)
            sbuf[t, k * cb:(k + 1) * cb] = back_ref[pl.ds(t * per + k * cb, cb)].astype(sbuf.dtype)
            copy(t, g, k).start()
    for k in range(chunks):
        for i in range(1, groups):
            copy(other(i), other(i), k).wait_recv()
        for b in range(k * cb, (k + 1) * cb):
            total = back_ref[g * per + b]
            for i in range(1, groups):
                total += rbuf[other(i), b].astype(jnp.float32)
            out_ref[:, b * width:(b + 1) * width] = total
    for k in range(chunks):
        for i in range(1, groups):
            copy(other(i), g, k).wait_send()


def exchange_call(groups, back):
    pblocks, probes, width = back.shape
    per = pblocks // groups
    chunks = min(4, per)
    vmem = pl.BlockSpec(memory_space=pltpu.VMEM)
    return pl.pallas_call(
        functools.partial(exchange_kernel, groups, chunks),
        out_shape=jax.ShapeDtypeStruct((probes, per * width), jnp.float32),
        in_specs=[vmem],
        out_specs=vmem,
        scratch_shapes=[
            pltpu.VMEM((groups, per, probes, width), jnp.bfloat16),
            pltpu.VMEM((groups, per, probes, width), jnp.bfloat16),
            pltpu.SemaphoreType.DMA((groups, chunks)),
            pltpu.SemaphoreType.DMA((groups, chunks)),
        ],
        compiler_params=pltpu.CompilerParams(
            collective_id=1, has_side_effects=True, vmem_limit_bytes=32 * 1024 * 1024),
        cost_estimate=pl.CostEstimate(flops=0, bytes_accessed=4 * back.size, transcendentals=0),
    )(back)


def on_device(groups, n, omega, blocks, bparam, bobs, count, weights):
    probes = omega.shape[0]
    width = blocks.shape[2]
    oblocks = weights.shape[1] // width
    pblocks = omega.shape[1] // width
    part = sparse_call(fwd_kernel, bparam, bobs, count, omega, blocks, oblocks, probes)
    scaled = reduce_call(n, part, weights)
    back = sparse_call(back_kernel, bparam, bobs, count, scaled, blocks, pblocks, probes)
    return exchange_call(groups, back)


def solution(mesh):
    in_specs = (
        P(None, "par"),
        P("grp", "par", None, None),
        P("grp", "par"),
        P("grp", "par"),
        P("grp", "par"),
        P("grp", None),
    )
    out_specs = P(None, ("par", "grp"))
    body = functools.partial(on_device, mesh.shape["grp"], mesh.shape["par"])
    return jax.shard_map(
        body, mesh=mesh, in_specs=in_specs, out_specs=out_specs, check_vma=False
    )
```

time: 171 us -> 49.5 us (0.29)
  waiting for transfers between devices: 116 us -> 0 us
  Pallas kernels: 0 us -> 43.2 us
  other arithmetic: 26.1 us -> 0 us
  between operations: 14.2 us -> 0.71 us
  matrix products: 10.7 us -> 0 us
    psum x1 -> x0, waiting for transfers between devices: 96 us -> none  [on_device(): fwd = lax.psum(partial_value, 'par')]
    pallas_call x0 -> x4, Pallas kernels: none -> 43.2 us  [the longest x1 28.9 us: reduce_call(): pl.pallas_call(functools.partial(reduce_kernel, n), out_shape=jax.ShapeDt...]
    scatter-add x2 -> x0, other arithmetic: 23.4 us -> none  [the longest x1 11.7 us: on_device(): local_terms = jax.ops.segment_sum(back, bparam, num_segments=pblocks)]
    reduce_scatter x1 -> x0, waiting for transfers between devices: 19.7 us -> none  [on_device(): return lax.psum_scatter(local_terms, 'grp', scatter_dimension=1, tiled=True)]
    dot_general x2 -> x0, matrix products: 10.7 us -> none  [the longest x1 5.88 us: on_device(): jnp.einsum('kco,cpo->ckp', pickv, blocks, preferred_element_type=jnp.floa...]
    unnamed x8 -> x13, local copies, waits for them, and re-layouts: 0.02 us -> 5.33 us
    reshape x3 -> x0, local copies, waits for them, and re-layouts: 2.25 us -> none  [the longest x1 1.1 us: on_device(): jnp.transpose(partial_value, (1, 0, 2)).reshape(probes, oblocks * width)]
  transfers between devices with their start and end apart: 2 -> 0, of which waited for: 2 -> 0; matrix products, arithmetic and copies ran while one was open for 0% -> 0% of each run, Pallas kernels for 0% -> 0%
where the time goes in v1:
time: 49.5 us; the launch traced here: 49.3 us
  Pallas kernels  43.2 us (87%)
  local copies, waits for them, and re-layouts  5.33 us (11%)
  between operations  0.71 us (1%)
    pallas_call x1, Pallas kernels, reduce_call(): pl.pallas_call(functools.partial(reduce_kernel, n), out_shape=jax.ShapeDt...  28.9 us
    pallas_call x1, Pallas kernels, exchange_call(): pl.pallas_call(functools.partial(exchange_kernel, groups, chunks), out_sh...  8.5 us
    pallas_call x2, Pallas kernels, sparse_call(): pl.pallas_call(kernel, out_shape=jax.ShapeDtypeStruct((outs, probes, widt...  5.81 us
    unnamed x13, local copies, waits for them, and re-layouts  5.33 us

profile of v1, /device:TPU:0, one launch (start us, length us, event | category | flops | bytes accessed | tf_op | source)
XLA Modules:
  0.0 49.3 jit_solution(16164118251264151579)
XLA Ops:
  0.7 0.0 copy-start
  0.7 2.2 %copy-done = bf16[1,128,128,128]{3,2,1,0:T(8,128)(2,1)S(1)} copy-done((bf16[1,128,128,128]{3,2,1,0:T(8,128)(2,1)S(1)}, bf16[1,128,128,128]{3,2,1,0:T(8,128)(2,1)}, u32[]{:S(2)}) %copy-start) | copy-done | bytes 4194328
  2.8 0.0 copy-start.2
  2.8 1.0 %copy-done.2 = bf16[32,8192]{1,0:T(8,128)(2,1)S(1)} copy-done((bf16[32,8192]{1,0:T(8,128)(2,1)S(1)}, bf16[32,8192]{1,0:T(8,128)(2,1)}, u32[]{:S(2)}) %copy-start.2) | copy-done | bytes 524312
  3.9 0.0 copy-start.4
  3.9 0.7 %copy-done.4 = s32[1,128]{1,0:T(1,128)S(1)} copy-done((s32[1,128]{1,0:T(1,128)S(1)}, s32[1,128]{1,0:T(1,128)}, u32[]{:S(2)}) %copy-start.4) | copy-done | bytes 536
  4.5 0.0 copy-start.5
  4.5 0.7 %copy-done.5 = s32[1,128]{1,0:T(1,128)S(1)} copy-done((s32[1,128]{1,0:T(1,128)S(1)}, s32[1,128]{1,0:T(1,128)}, u32[]{:S(2)}) %copy-start.5) | copy-done | bytes 536
  5.2 0.0 copy-start.3
  5.2 0.0 copy-start.1
  5.2 2.4 %shard_map.64.part_ref = f32[64,32,128]{2,1,0:T(8,128)S(1)} custom-call(s32[1,128]{1,0:T(1,128)S(1)} %copy-done.4, s32[1,128]{1,0:T(1,128)S(1)} %copy-done.5, s32[1,1]{1,0:T(1,128)S(6)} %copy.8.count, bf16[32,8192]{1,0:T(8,128)(2,1)S(1)} %copy-done.2, bf16[1,128,128,128]{3,2,1,0:T(8,128)(2,1)S(1)} %copy-done), custom_call_target="tpu_custom_call" | custom-call | flops 134217728 | bytes 4194304 | tf_op jit(solution)/shard_map/pallas_call | solution.py:63
  7.6 0.0 copy-done.3
  7.6 28.9 %shard_map.65.scaled_ref = bf16[64,32,128]{2,1,0:T(8,128)(2,1)S(1)} custom-call(f32[64,32,128]{2,1,0:T(8,128)S(1)} %shard_map.64.part_ref, f32[1,8192]{1,0:T(1,128)S(1)} %copy-done.3), custom_call_target="tpu_custom_call" | custom-call | bytes 1048576 | tf_op jit(solution)/shard_map/pallas_call | solution.py:192
  36.6 0.0 copy-done.1
  36.6 3.4 %shard_map.66.back_ref = f32[64,32,128]{2,1,0:T(8,128)S(1)} custom-call(s32[1,128]{1,0:T(1,128)S(1)} %copy-done.4, s32[1,128]{1,0:T(1,128)S(1)} %copy-done.5, s32[1,1]{1,0:T(1,128)S(6)} %copy.8.count, bf16[64,32,128]{2,1,0:T(8,128)(2,1)S(1)} %shard_map.65.scaled_ref, bf16[1,128,128,128]{3,2,1,0:T(8,128)(2,1)S(1)} %copy-done.1), custom_call_target="tpu_custom_call" | custom-call | flops 134217728 | bytes 4194304 | tf_op jit(solution)/shard_map/pallas_call | solution.py:63
  40.0 8.5 %shard_map.67 = f32[32,4096]{1,0:T(8,128)S(1)} custom-call(f32[64,32,128]{2,1,0:T(8,128)S(1)} %shard_map.66.back_ref), custom_call_target="tpu_custom_call" | custom-call | bytes 1048576 | tf_op jit(solution)/shard_map/pallas_call | solution.py:251
  48.5 0.8 %copy.9 = f32[32,4096]{1,0:T(8,128)} copy(f32[32,4096]{1,0:T(8,128)S(1)} %shard_map.67) | data formatting | bytes 1048576
Async XLA Ops:
  0.7 2.2 %copy-start = (bf16[1,128,128,128]{3,2,1,0:T(8,128)(2,1)S(1)}, bf16[1,128,128,128]{3,2,1,0:T(8,128)(2,1)}, u32[]{:S(2)}) copy-start(bf16[1,128,128,128]{3,2,1,0:T(8,128)(2,1)} %blocks_ref.3) | copy-start | bytes 12582916
  2.8 1.0 %copy-start.2 = (bf16[32,8192]{1,0:T(8,128)(2,1)S(1)}, bf16[32,8192]{1,0:T(8,128)(2,1)}, u32[]{:S(2)}) copy-start(bf16[32,8192]{1,0:T(8,128)(2,1)} %omega_ref.1) | copy-start | bytes 1572868
  3.9 0.7 %copy-start.4 = (s32[1,128]{1,0:T(1,128)S(1)}, s32[1,128]{1,0:T(1,128)}, u32[]{:S(2)}) copy-start(s32[1,128]{1,0:T(1,128)} %bparam.3) | copy-start | bytes 1540
  4.5 0.7 %copy-start.5 = (s32[1,128]{1,0:T(1,128)S(1)}, s32[1,128]{1,0:T(1,128)}, u32[]{:S(2)}) copy-start(s32[1,128]{1,0:T(1,128)} %bobs.3) | copy-start | bytes 1540
  5.2 2.4 %copy-start.3 = (f32[1,8192]{1,0:T(1,128)S(1)}, f32[1,8192]{1,0:T(1,128)}, u32[]{:S(2)}) copy-start(f32[1,8192]{1,0:T(1,128)} %weight_ref.1) | copy-start | bytes 98308
  5.2 31.4 %copy-start.1 = (bf16[1,128,128,128]{3,2,1,0:T(8,128)(2,1)S(1)}, bf16[1,128,128,128]{3,2,1,0:T(8,128)(2,1)}, u32[]{:S(2)}) copy-start(bf16[1,128,128,128]{3,2,1,0:T(8,128)(2,1)} %blocks_ref.3) | copy-start | bytes 12582916

commit v2 on v1

v2 whole, which is shorter than its diff:
```python
import functools

import jax
import jax.numpy as jnp
from jax import lax
from jax.experimental import pallas as pl
from jax.experimental.pallas import tpu as pltpu
from jax.sharding import PartitionSpec as P

MESH = pl.DeviceIdType.MESH
STEP = 32
LEVELS = 32000.0
VMEM_LIMIT = 16 * 1024 * 1024


def fwd_kernel(bparam, bobs, count, omega, blocks, acc):
    oblocks = acc.shape[0] - 1
    slots, width = blocks.shape[1], blocks.shape[2]
    acc[...] = jnp.zeros_like(acc)

    def step(i, carry):
        for j in range(STEP):
            s = i * STEP + j
            to = jnp.where(s < count[0, 0], bobs[0, s], oblocks)
            at = pl.multiple_of(bparam[0, s] * width, width)
            acc[to] += jnp.dot(
                omega[:, pl.ds(at, width)], blocks[0, s], preferred_element_type=jnp.float32
            )
        return carry

    lax.fori_loop(0, slots // STEP, step, 0)


def fwd_call(bparam, bobs, count, omega, blocks, oblocks):
    probes = omega.shape[0]
    slots, width = blocks.shape[1], blocks.shape[2]
    smem = pl.BlockSpec(memory_space=pltpu.SMEM)
    vmem = pl.BlockSpec(memory_space=pltpu.VMEM)
    return pl.pallas_call(
        fwd_kernel,
        out_shape=jax.ShapeDtypeStruct((oblocks + 1, probes, width), jnp.float32),
        in_specs=[smem, smem, smem, vmem, vmem],
        out_specs=vmem,
        compiler_params=pltpu.CompilerParams(vmem_limit_bytes=VMEM_LIMIT),
        cost_estimate=pl.CostEstimate(
            flops=2 * slots * probes * width * width,
            bytes_accessed=2 * slots * width * width, transcendentals=0),
    )(bparam, bobs, count, omega, blocks)


def back_kernel(bparam, bobs, count, scaled_ref, blocks_ref, acc):
    pblocks = acc.shape[0] - 1
    slots = blocks_ref.shape[1]
    acc[...] = jnp.zeros_like(acc)

    def step(i, carry):
        for j in range(STEP):
            s = i * STEP + j
            to = jnp.where(s < count[0, 0], bparam[0, s], pblocks)
            acc[to] += lax.dot_general(
                scaled_ref[bobs[0, s]], blocks_ref[0, s],
                (((1,), (1,)), ((), ())), preferred_element_type=jnp.float32)
        return carry

    lax.fori_loop(0, slots // (STEP), step, 0)


def back_call(bparam, bobs, count, scaled, blocks, pblocks):
    probes = scaled.shape[1]
    slots, width = blocks.shape[1], blocks.shape[2]
    smem = pl.BlockSpec(memory_space=pltpu.SMEM)
    vmem = pl.BlockSpec(memory_space=pltpu.VMEM)
    return pl.pallas_call(
        back_kernel,
        out_shape=jax.ShapeDtypeStruct((pblocks + 1, probes, width), jnp.float32),
        in_specs=[smem, smem, smem, vmem, vmem],
        out_specs=vmem,
        compiler_params=pltpu.CompilerParams(vmem_limit_bytes=VMEM_LIMIT),
        cost_estimate=pl.CostEstimate(
            flops=2 * slots * probes * width * width,
            bytes_accessed=2 * slots * width * width, transcendentals=0),
    )(bparam, bobs, count, scaled, blocks)


def reduce_kernel(
    n, part_ref, weight_ref, out_ref, sib, sbuf, rbuf, sscale, rscale,
    s1, r1, s2, r2, s3, r3, s4, r4, s5, r5, s6,
):
    me = lax.axis_index("par")
    chips = n // 2
    rows = 2
    cols = chips // rows
    q, c = me // 2, lax.rem(me, 2)
    z, y = q // rows, lax.rem(q, rows)
    oblocks, width = out_ref.shape[0], out_ref.shape[2]
    half = oblocks // 2
    nb = half // chips
    mate = {"par": 2 * q + 1 - c}
    beside = rows * z + 1 - y

    def chip(i):
        return lax.rem(q + i, chips)

    def in_row(i):
        return rows * lax.rem(z + i, cols) + y

    def in_other_row(i):
        return rows * lax.rem(z + i, cols) + 1 - y

    def peer(t):
        return {"par": 2 * t + c}

    def mine(t):
        return pl.ds(c * half + t * nb, nb)

    def theirs(t):
        return pl.ds((1 - c) * half + t * nb, nb)

    barrier = pltpu.get_barrier_semaphore()
    pl.semaphore_signal(barrier, inc=1, device_id=mate, device_id_type=MESH)
    for i in range(1, chips):
        pl.semaphore_signal(barrier, inc=1, device_id=peer(chip(i)), device_id_type=MESH)
    pl.semaphore_wait(barrier, chips)

    def remote(src, dst, send, recv, device):
        return pltpu.make_async_remote_copy(
            src_ref=src, dst_ref=dst, send_sem=send, recv_sem=recv,
            device_id=device, device_id_type=MESH)

    def to_mate(t):
        return remote(part_ref.at[theirs(t)], sib.at[t], s1.at[t], r1.at[t], mate)

    def to_owner(t, lands):
        return remote(sbuf.at[t], rbuf.at[lands], s2.at[t], r2.at[lands], peer(t))

    def scale_to_owner(t, lands):
        return remote(sscale.at[t], rscale.at[lands], s5.at[t], r5.at[lands], peer(t))

    def gather(piece, to, sems, at):
        return remote(
            out_ref.at[mine(piece)], out_ref.at[mine(piece)], sems.at[at], r3.at[piece], peer(to))

    def hand_over(t):
        return remote(out_ref.at[mine(t)], out_ref.at[mine(t)], s4.at[t], r4.at[t], mate)

    def take_over(t):
        return remote(out_ref.at[theirs(t)], out_ref.at[theirs(t)], s4.at[t], r4.at[t], mate)

    for i in range(1, chips + 1):
        to_mate(chip(i)).start()
    for i in range(1, chips):
        t = chip(i)
        to_mate(t).wait_recv()
        value = part_ref[mine(t)] + sib[t]
        largest = jnp.max(jnp.max(jnp.abs(value), axis=0), axis=0, keepdims=True)
        largest = jnp.maximum(largest, 1e-30)
        sscale[t] = jnp.broadcast_to(largest * (1.0 / LEVELS), sscale.shape[1:])
        scale_to_owner(t, q).start()
        level = jnp.round(value * (LEVELS / largest)[None])
        sbuf[t] = level.astype(jnp.int32).astype(sbuf.dtype)
        to_owner(t, q).start()
    to_mate(q).wait_recv()
    total = part_ref[mine(q)] + sib[q]
    for i in range(1, chips):
        t = chip(chips - i)
        scale_to_owner(t, t).wait_recv()
        to_owner(t, t).wait_recv()
        level = rbuf[t].astype(jnp.int32).astype(jnp.float32)
        total += level * rscale[t][0:1][None]
    for b in range(nb):
        block = c * half + q * nb + b
        weight = weight_ref[0:1, pl.ds(pl.multiple_of(block * width, width), width)]
        out_ref[block] = (total[b] * weight).astype(out_ref.dtype)

    gather(q, beside, s6, q).start()
    for i in range(1, cols):
        gather(q, in_row(i), s3, in_row(i)).start()
    hand_over(q).start()
    for i in range(1, cols):
        t = in_row(cols - i)
        gather(t, t, s3, t).wait_recv()
        gather(t, beside, s6, t).start()
        hand_over(t).start()
    for i in range(cols):
        t = in_other_row((cols - i) % cols)
        gather(t, t, s3, t).wait_recv()
        hand_over(t).start()
    for i in range(chips):
        take_over(chip(i)).wait_recv()
    for i in range(chips):
        t = chip(i)
        to_mate(t).wait_send()
        hand_over(t).wait_send()
    for i in range(1, chips):
        t = chip(i)
        to_owner(t, q).wait_send()
        scale_to_owner(t, q).wait_send()
    for i in range(cols):
        gather(in_row(i), beside, s6, in_row(i)).wait_send()
    for i in range(1, cols):
        gather(q, in_row(i), s3, in_row(i)).wait_send()


def reduce_call(n, part, weights):
    oblocks, probes, width = part.shape[0] - 1, part.shape[1], part.shape[2]
    chips = n // 2
    nb = oblocks // n
    dma = pltpu.SemaphoreType.DMA((chips,))
    vmem = pl.BlockSpec(memory_space=pltpu.VMEM)
    return pl.pallas_call(
        functools.partial(reduce_kernel, n),
        out_shape=jax.ShapeDtypeStruct((oblocks, probes, width), jnp.bfloat16),
        in_specs=[vmem, vmem],
        out_specs=vmem,
        scratch_shapes=[
            pltpu.VMEM((chips, nb, probes, width), jnp.float32),
            pltpu.VMEM((chips, nb, probes, width), jnp.int16),
            pltpu.VMEM((chips, nb, probes, width), jnp.int16),
            pltpu.VMEM((chips, 8, width), jnp.float32),
            pltpu.VMEM((chips, 8, width), jnp.float32),
        ] + [dma] * 11,
        compiler_params=pltpu.CompilerParams(
            collective_id=0, has_side_effects=True, vmem_limit_bytes=VMEM_LIMIT),
        cost_estimate=pl.CostEstimate(flops=0, bytes_accessed=4 * part.size, transcendentals=0),
    )(part, weights)


def exchange_kernel(groups, chunks, back_ref, out_ref, sbuf, rbuf, ss, rs):
    g = lax.axis_index("grp")
    pblocks, width = back_ref.shape[0] - 1, back_ref.shape[2]
    per = pblocks // groups
    cb = per // chunks

    def other(i):
        return lax.rem(g + i, groups)

    def copy(t, lands, k):
        return pltpu.make_async_remote_copy(
            src_ref=sbuf.at[t, pl.ds(k * cb, cb)], dst_ref=rbuf.at[lands, pl.ds(k * cb, cb)],
            send_sem=ss.at[t, k], recv_sem=rs.at[lands, k],
            device_id={"grp": t}, device_id_type=MESH)

    barrier = pltpu.get_barrier_semaphore()
    for i in range(1, groups):
        pl.semaphore_signal(barrier, inc=1, device_id={"grp": other(i)}, device_id_type=MESH)
    pl.semaphore_wait(barrier, groups - 1)

    for k in range(chunks):
        for i in range(1, groups):
            t = other(i)
            sbuf[t, k * cb:(k + 1) * cb] = back_ref[pl.ds(t * per + k * cb, cb)].astype(sbuf.dtype)
            copy(t, g, k).start()
    for k in range(chunks):
        for i in range(1, groups):
            copy(other(i), other(i), k).wait_recv()
        for b in range(k * cb, (k + 1) * cb):
            total = back_ref[g * per + b]
            for i in range(1, groups):
                total += rbuf[other(i), b].astype(jnp.float32)
            out_ref[:, b * width:(b + 1) * width] = total
    for k in range(chunks):
        for i in range(1, groups):
            copy(other(i), g, k).wait_send()


def exchange_call(groups, back):
    pblocks, probes, width = back.shape[0] - 1, back.shape[1], back.shape[2]
    per = pblocks // groups
    chunks = min(4, per)
    vmem = pl.BlockSpec(memory_space=pltpu.VMEM)
    return pl.pallas_call(
        functools.partial(exchange_kernel, groups, chunks),
        out_shape=jax.ShapeDtypeStruct((probes, per * width), jnp.float32),
        in_specs=[vmem],
        out_specs=vmem,
        scratch_shapes=[
            pltpu.VMEM((groups, per, probes, width), jnp.bfloat16),
            pltpu.VMEM((groups, per, probes, width), jnp.bfloat16),
            pltpu.SemaphoreType.DMA((groups, chunks)),
            pltpu.SemaphoreType.DMA((groups, chunks)),
        ],
        compiler_params=pltpu.CompilerParams(
            collective_id=1, has_side_effects=True, vmem_limit_bytes=VMEM_LIMIT),
        cost_estimate=pl.CostEstimate(flops=0, bytes_accessed=4 * back.size, transcendentals=0),
    )(back)


def on_device(groups, n, omega, blocks, bparam, bobs, count, weights):
    width = blocks.shape[2]
    oblocks = weights.shape[1] // width
    pblocks = omega.shape[1] // width
    part = fwd_call(bparam, bobs, count, omega, blocks, oblocks)
    scaled = reduce_call(n, part, weights)
    back = back_call(bparam, bobs, count, scaled, blocks, pblocks)
    return exchange_call(groups, back)


def solution(mesh):
    in_specs = (
        P(None, "par"),
        P("grp", "par", None, None),
        P("grp", "par"),
        P("grp", "par"),
        P("grp", "par"),
        P("grp", None),
    )
    out_specs = P(None, ("par", "grp"))
    body = functools.partial(on_device, mesh.shape["grp"], mesh.shape["par"])
    return jax.shard_map(
        body, mesh=mesh, in_specs=in_specs, out_specs=out_specs, check_vma=False
    )
```

time: 49.5 us -> 45.6 us (0.921)
  Pallas kernels: 43.2 us -> 39.5 us
    pallas_call x1, Pallas kernels: 28.9 us -> 25.1 us  [reduce_call(): pl.pallas_call(functools.partial(reduce_kernel, n), out_shape=jax.ShapeDt...]
where the time goes in v2:
time: 45.6 us; the launch traced here: 45.5 us
  Pallas kernels  39.5 us (87%)
  local copies, waits for them, and re-layouts  5.33 us (12%)
  between operations  0.7 us (2%)
    pallas_call x1, Pallas kernels, reduce_call(): pl.pallas_call(functools.partial(reduce_kernel, n), out_shape=jax.ShapeDt...  25.1 us
    pallas_call x1, Pallas kernels, exchange_call(): pl.pallas_call(functools.partial(exchange_kernel, groups, chunks), out_sh...  8.84 us
    unnamed x13, local copies, waits for them, and re-layouts  5.33 us
    pallas_call x1, Pallas kernels, back_call(): pl.pallas_call(back_kernel, out_shape=jax.ShapeDtypeStruct((pblocks + 1,...  3.26 us
    pallas_call x1, Pallas kernels, fwd_call(): pl.pallas_call(fwd_kernel, out_shape=jax.ShapeDtypeStruct((oblocks + 1, p...  2.21 us

profile of v2, /device:TPU:0, one launch (start us, length us, event | category | flops | bytes accessed | tf_op | source)
XLA Modules:
  0.0 45.5 jit_solution(2590396284060433223)
XLA Ops:
  0.7 0.0 copy-start
  0.7 2.2 %copy-done = bf16[1,128,128,128]{3,2,1,0:T(8,128)(2,1)S(1)} copy-done((bf16[1,128,128,128]{3,2,1,0:T(8,128)(2,1)S(1)}, bf16[1,128,128,128]{3,2,1,0:T(8,128)(2,1)}, u32[]{:S(2)}) %copy-start) | copy-done | bytes 4194328
  2.8 0.0 copy-start.2
  2.8 1.0 %copy-done.2 = bf16[32,8192]{1,0:T(8,128)(2,1)S(1)} copy-done((bf16[32,8192]{1,0:T(8,128)(2,1)S(1)}, bf16[32,8192]{1,0:T(8,128)(2,1)}, u32[]{:S(2)}) %copy-start.2) | copy-done | bytes 524312
  3.9 0.0 copy-start.4
  3.9 0.7 %copy-done.4 = s32[1,128]{1,0:T(1,128)S(1)} copy-done((s32[1,128]{1,0:T(1,128)S(1)}, s32[1,128]{1,0:T(1,128)}, u32[]{:S(2)}) %copy-start.4) | copy-done | bytes 536
  4.5 0.0 copy-start.5
  4.5 0.7 %copy-done.5 = s32[1,128]{1,0:T(1,128)S(1)} copy-done((s32[1,128]{1,0:T(1,128)S(1)}, s32[1,128]{1,0:T(1,128)}, u32[]{:S(2)}) %copy-start.5) | copy-done | bytes 536
  5.2 0.0 copy-start.3
  5.2 0.0 copy-start.1
  5.2 2.2 %shard_map.64.part_ref = f32[65,32,128]{2,1,0:T(8,128)S(1)} custom-call(s32[1,128]{1,0:T(1,128)S(1)} %copy-done.4, s32[1,128]{1,0:T(1,128)S(1)} %copy-done.5, s32[1,1]{1,0:T(1,128)S(6)} %copy.8.count, bf16[32,8192]{1,0:T(8,128)(2,1)S(1)} %copy-done.2, bf16[1,128,128,128]{3,2,1,0:T(8,128)(2,1)S(1)} %copy-done), custom_call_target="tpu_custom_call" | custom-call | flops 134217728 | bytes 4194304 | tf_op jit(solution)/shard_map/pallas_call | solution.py:39
  7.4 0.0 copy-done.3
  7.4 25.1 %shard_map.65.scaled_ref = bf16[64,32,128]{2,1,0:T(8,128)(2,1)S(1)} custom-call(f32[65,32,128]{2,1,0:T(8,128)S(1)} %shard_map.64.part_ref, f32[1,8192]{1,0:T(1,128)S(1)} %copy-done.3), custom_call_target="tpu_custom_call" | custom-call | bytes 1064960 | tf_op jit(solution)/shard_map/pallas_call | solution.py:210
  32.6 0.0 copy-done.1
  32.6 3.3 %shard_map.66.back_ref = f32[65,32,128]{2,1,0:T(8,128)S(1)} custom-call(s32[1,128]{1,0:T(1,128)S(1)} %copy-done.4, s32[1,128]{1,0:T(1,128)S(1)} %copy-done.5, s32[1,1]{1,0:T(1,128)S(6)} %copy.8.count, bf16[64,32,128]{2,1,0:T(8,128)(2,1)S(1)} %shard_map.65.scaled_ref, bf16[1,128,128,128]{3,2,1,0:T(8,128)(2,1)S(1)} %copy-done.1), custom_call_target="tpu_custom_call" | custom-call | flops 134217728 | bytes 4194304 | tf_op jit(solution)/shard_map/pallas_call | solution.py:73
  35.8 8.8 %shard_map.67 = f32[32,4096]{1,0:T(8,128)S(1)} custom-call(f32[65,32,128]{2,1,0:T(8,128)S(1)} %shard_map.66.back_ref), custom_call_target="tpu_custom_call" | custom-call | bytes 1064960 | tf_op jit(solution)/shard_map/pallas_call | solution.py:271
  44.7 0.8 %copy.9 = f32[32,4096]{1,0:T(8,128)} copy(f32[32,4096]{1,0:T(8,128)S(1)} %shard_map.67) | data formatting | bytes 1048576
Async XLA Ops:
  0.7 2.2 %copy-start = (bf16[1,128,128,128]{3,2,1,0:T(8,128)(2,1)S(1)}, bf16[1,128,128,128]{3,2,1,0:T(8,128)(2,1)}, u32[]{:S(2)}) copy-start(bf16[1,128,128,128]{3,2,1,0:T(8,128)(2,1)} %blocks_ref.1) | copy-start | bytes 12582916
  2.8 1.0 %copy-start.2 = (bf16[32,8192]{1,0:T(8,128)(2,1)S(1)}, bf16[32,8192]{1,0:T(8,128)(2,1)}, u32[]{:S(2)}) copy-start(bf16[32,8192]{1,0:T(8,128)(2,1)} %omega.1) | copy-start | bytes 1572868
  3.9 0.7 %copy-start.4 = (s32[1,128]{1,0:T(1,128)S(1)}, s32[1,128]{1,0:T(1,128)}, u32[]{:S(2)}) copy-start(s32[1,128]{1,0:T(1,128)} %bparam.3) | copy-start | bytes 1540
  4.5 0.7 %copy-start.5 = (s32[1,128]{1,0:T(1,128)S(1)}, s32[1,128]{1,0:T(1,128)}, u32[]{:S(2)}) copy-start(s32[1,128]{1,0:T(1,128)} %bobs.3) | copy-start | bytes 1540
  5.2 2.2 %copy-start.3 = (f32[1,8192]{1,0:T(1,128)S(1)}, f32[1,8192]{1,0:T(1,128)}, u32[]{:S(2)}) copy-start(f32[1,8192]{1,0:T(1,128)} %weight_ref.1) | copy-start | bytes 98308
  5.2 27.4 %copy-start.1 = (bf16[1,128,128,128]{3,2,1,0:T(8,128)(2,1)S(1)}, bf16[1,128,128,128]{3,2,1,0:T(8,128)(2,1)}, u32[]{:S(2)}) copy-start(bf16[1,128,128,128]{3,2,1,0:T(8,128)(2,1)} %blocks_ref.1) | copy-start | bytes 12582916

commit v3 on v0

v3 whole, which is shorter than its diff:
```python
import functools

import jax
import jax.numpy as jnp
from jax import lax
from jax.experimental import pallas as pl
from jax.experimental.pallas import tpu as pltpu
from jax.sharding import PartitionSpec as P

MESH = pl.DeviceIdType.MESH
STEP = 16
ROWS = 16
LEVELS = 32000.0
VMEM_LIMIT = 57 * 1024 * 1024


def kernel(
    n, groups,
    bparam_hbm, bobs_hbm, count, omega_hbm, blocks_hbm, weight_hbm, out_ref,
    bparam, bobs, bparam_row, bobs_row, omega, panels, weight, blocks,
    terms, part, scaled, sib, sbuf, rbuf, sscale, rscale, own, half_out, xsend, xrecv,
    small, big, s1, r1, s2, r2, s3, r3, s4, r4, s5, r5, s6, sx, rx,
):
    me = lax.axis_index("par")
    g = lax.axis_index("grp")
    probes = omega.shape[0]
    slots, width = blocks.shape[0], blocks.shape[1]
    oblocks = weight.shape[1] // width
    pblocks = omega.shape[1] // width
    per = pblocks // groups
    chips = n // 2
    rows = 2
    cols = chips // rows
    q, c = me // 2, lax.rem(me, 2)
    z, y = q // rows, lax.rem(q, rows)
    half = oblocks // 2
    nb = half // chips
    mate = {"par": 2 * q + 1 - c}
    beside = rows * z + 1 - y

    def chip(i):
        return lax.rem(q + i, chips)

    def in_row(i):
        return rows * lax.rem(z + i, cols) + y

    def in_other_row(i):
        return rows * lax.rem(z + i, cols) + 1 - y

    def peer(t):
        return {"par": 2 * t + c}

    def other(i):
        return lax.rem(g + i, groups)

    def lines(block, count_of):
        return pl.ds(pl.multiple_of(block * probes, probes), count_of * probes)

    def mine(t):
        return pl.ds(c * half + t * nb, nb)

    def theirs(t):
        return pl.ds((1 - c) * half + t * nb, nb)

    early = [
        pltpu.make_async_copy(bparam_hbm, bparam, small.at[0]),
        pltpu.make_async_copy(bobs_hbm, bobs, small.at[1]),
        pltpu.make_async_copy(omega_hbm, omega, small.at[2]),
        pltpu.make_async_copy(bparam_hbm, bparam_row, small.at[3]),
        pltpu.make_async_copy(bobs_hbm, bobs_row, small.at[4]),
        pltpu.make_async_copy(weight_hbm, weight, small.at[5]),
    ]

    def blocks_of(i):
        at = pl.ds(i * STEP, STEP)
        return pltpu.make_async_copy(blocks_hbm.at[0, at], blocks.at[at], big.at[i])

    for copy in early:
        copy.start()
    for i in range(slots // STEP):
        blocks_of(i).start()

    barrier = pltpu.get_barrier_semaphore()
    pl.semaphore_signal(barrier, inc=1, device_id=mate, device_id_type=MESH)
    for i in range(1, chips):
        pl.semaphore_signal(barrier, inc=1, device_id=peer(chip(i)), device_id_type=MESH)
    for i in range(1, groups):
        pl.semaphore_signal(barrier, inc=1, device_id={"grp": other(i)}, device_id_type=MESH)

    for copy in early:
        copy.wait()
    for b in range(pblocks):
        panels[b] = omega[:, b * width:(b + 1) * width]

    def fwd_step(i, carry):
        blocks_of(i).wait()
        for j in range(STEP):
            s = i * STEP + j
            terms[lines(s, 1)] = jnp.dot(
                panels[bparam[0, s]], blocks[s], preferred_element_type=jnp.float32)
        return carry

    lax.fori_loop(0, slots // STEP, fwd_step, 0)

    used = lax.broadcasted_iota(jnp.int32, (1, slots), 1) < count[0, 0]

    def chooser(row, first, length):
        place = lax.broadcasted_iota(jnp.int32, (length, slots), 0) + first
        chosen = jnp.where((place == row) & used, 1.0, 0.0).astype(jnp.bfloat16)
        return jnp.concatenate([chosen, chosen], axis=1)

    def summed(chosen, k):
        value = terms[pl.ds(k, slots, stride=probes), :]
        high = value.astype(jnp.bfloat16)
        low = (value - high.astype(jnp.float32)).astype(jnp.bfloat16)
        return jnp.dot(
            chosen, jnp.concatenate([high, low], axis=0), preferred_element_type=jnp.float32)

    by_obs = chooser(bobs_row[...], 0, oblocks)
    for k in range(probes):
        part[pl.ds(k, oblocks, stride=probes), :] = summed(by_obs, k)

    def remote(src, dst, send, recv, device):
        return pltpu.make_async_remote_copy(
            src_ref=src, dst_ref=dst, send_sem=send, recv_sem=recv,
            device_id=device, device_id_type=MESH)

    def to_mate(t):
        return remote(
            part.at[lines((1 - c) * half + t * nb, nb)], sib.at[t], s1.at[t], r1.at[t], mate)

    def to_owner(t, lands):
        return remote(sbuf.at[t], rbuf.at[lands], s2.at[t], r2.at[lands], peer(t))

    def scale_to_owner(t, lands):
        return remote(sscale.at[t], rscale.at[lands], s5.at[t], r5.at[lands], peer(t))

    def gather(piece, to, sems, at):
        return remote(
            scaled.at[mine(piece)], scaled.at[mine(piece)], sems.at[at], r3.at[piece], peer(to))

    def hand_over(t):
        return remote(scaled.at[mine(t)], scaled.at[mine(t)], s4.at[t], r4.at[t], mate)

    def take_over(t):
        return remote(scaled.at[theirs(t)], scaled.at[theirs(t)], s4.at[t], r4.at[t], mate)

    pl.semaphore_wait(barrier, chips + groups - 1)
    for i in range(1, chips + 1):
        to_mate(chip(i)).start()
    for i in range(1, chips):
        t = chip(i)
        to_mate(t).wait_recv()
        value = part[lines(c * half + t * nb, nb), :] + sib[t]
        largest = jnp.max(jnp.abs(value), axis=0, keepdims=True)
        largest = jnp.maximum(largest, 1e-30)
        sscale[t] = jnp.broadcast_to(largest * (1.0 / LEVELS), sscale.shape[1:])
        scale_to_owner(t, q).start()
        level = jnp.round(value * (LEVELS / largest))
        sbuf[t] = level.astype(jnp.int32).astype(sbuf.dtype)
        to_owner(t, q).start()
    to_mate(q).wait_recv()
    total = part[lines(c * half + q * nb, nb), :] + sib[q]
    for i in range(1, chips):
        t = chip(chips - i)
        scale_to_owner(t, t).wait_recv()
        to_owner(t, t).wait_recv()
        total += rbuf[t].astype(jnp.int32).astype(jnp.float32) * rscale[t][0:1]
    for b in range(nb):
        block = c * half + q * nb + b
        factor = weight[0:1, pl.ds(pl.multiple_of(block * width, width), width)]
        scaled[block] = (total[b * probes:(b + 1) * probes] * factor).astype(scaled.dtype)

    gather(q, beside, s6, q).start()
    for i in range(1, cols):
        gather(q, in_row(i), s3, in_row(i)).start()
    hand_over(q).start()
    for i in range(1, cols):
        t = in_row(cols - i)
        gather(t, t, s3, t).wait_recv()
        gather(t, beside, s6, t).start()
        hand_over(t).start()
    for i in range(cols):
        t = in_other_row((cols - i) % cols)
        gather(t, t, s3, t).wait_recv()
        hand_over(t).start()
    for i in range(chips):
        take_over(chip(i)).wait_recv()

    def back_step(i, carry):
        for j in range(STEP):
            s = i * STEP + j
            terms[lines(s, 1)] = lax.dot_general(
                scaled[bobs[0, s]], blocks[s],
                (((1,), (1,)), ((), ())), preferred_element_type=jnp.float32)
        return carry

    lax.fori_loop(0, slots // STEP, back_step, 0)

    def exchange(t, lands, h):
        return remote(
            xsend.at[t, h], xrecv.at[lands, h], sx.at[t, h], rx.at[lands, h], {"grp": t})

    parts = probes // ROWS
    for i in range(1, groups):
        t = other(i)
        chosen = chooser(bparam_row[...], t * per, per)
        for h in range(parts):
            for k in range(ROWS):
                half_out[pl.ds(k, per, stride=ROWS), :] = summed(chosen, h * ROWS + k)
            xsend[t, h] = half_out[...].astype(xsend.dtype)
            exchange(t, g, h).start()
    chosen = chooser(bparam_row[...], g * per, per)
    for k in range(probes):
        own[pl.ds(k, per, stride=probes), :] = summed(chosen, k)
    for h in range(parts):
        for i in range(1, groups):
            exchange(other(i), other(i), h).wait_recv()
        for b in range(per):
            value = own[b * probes + h * ROWS:b * probes + (h + 1) * ROWS, :]
            for i in range(1, groups):
                value += xrecv[other(i), h, b * ROWS:(b + 1) * ROWS, :].astype(jnp.float32)
            out_ref[h * ROWS:(h + 1) * ROWS, b * width:(b + 1) * width] = value

    for i in range(chips):
        t = chip(i)
        to_mate(t).wait_send()
        hand_over(t).wait_send()
    for i in range(1, chips):
        t = chip(i)
        to_owner(t, q).wait_send()
        scale_to_owner(t, q).wait_send()
    for i in range(cols):
        gather(in_row(i), beside, s6, in_row(i)).wait_send()
    for i in range(1, cols):
        gather(q, in_row(i), s3, in_row(i)).wait_send()
    for i in range(1, groups):
        for h in range(parts):
            exchange(other(i), g, h).wait_send()


def on_device(groups, n, omega, blocks, bparam, bobs, count, weights):
    probes = omega.shape[0]
    slots, width = blocks.shape[1], blocks.shape[2]
    oblocks = weights.shape[1] // width
    pblocks = omega.shape[1] // width
    per = pblocks // groups
    chips = n // 2
    piece = oblocks // n * probes
    parts = probes // ROWS
    dma = pltpu.SemaphoreType.DMA
    hbm = pl.BlockSpec(memory_space=pl.ANY)
    return pl.pallas_call(
        functools.partial(kernel, n, groups),
        out_shape=jax.ShapeDtypeStruct((probes, per * width), jnp.float32),
        in_specs=[hbm, hbm, pl.BlockSpec(memory_space=pltpu.SMEM), hbm, hbm, hbm],
        out_specs=pl.BlockSpec(memory_space=pltpu.VMEM),
        scratch_shapes=[
            pltpu.SMEM(bparam.shape, jnp.int32),
            pltpu.SMEM(bobs.shape, jnp.int32),
            pltpu.VMEM(bparam.shape, jnp.int32),
            pltpu.VMEM(bobs.shape, jnp.int32),
            pltpu.VMEM(omega.shape, omega.dtype),
            pltpu.VMEM((pblocks, probes, width), omega.dtype),
            pltpu.VMEM(weights.shape, weights.dtype),
            pltpu.VMEM(blocks.shape[1:], blocks.dtype),
            pltpu.VMEM((slots * probes, width), jnp.float32),
            pltpu.VMEM((oblocks * probes, width), jnp.float32),
            pltpu.VMEM((oblocks, probes, width), jnp.bfloat16),
            pltpu.VMEM((chips, piece, width), jnp.float32),
            pltpu.VMEM((chips, piece, width), jnp.int16),
            pltpu.VMEM((chips, piece, width), jnp.int16),
            pltpu.VMEM((chips, 8, width), jnp.float32),
            pltpu.VMEM((chips, 8, width), jnp.float32),
            pltpu.VMEM((per * probes, width), jnp.float32),
            pltpu.VMEM((per * ROWS, width), jnp.float32),
            pltpu.VMEM((groups, parts, per * ROWS, width), jnp.bfloat16),
            pltpu.VMEM((groups, parts, per * ROWS, width), jnp.bfloat16),
            dma((6,)),
            dma((slots // STEP,)),
        ] + [dma((chips,))] * 11 + [dma((groups, parts))] * 2,
        compiler_params=pltpu.CompilerParams(
            collective_id=0, has_side_effects=True, vmem_limit_bytes=VMEM_LIMIT),
        cost_estimate=pl.CostEstimate(
            flops=4 * slots * probes * width * width,
            bytes_accessed=2 * slots * width * width, transcendentals=0),
    )(bparam, bobs, count, omega, blocks, weights)


def solution(mesh):
    in_specs = (
        P(None, "par"),
        P("grp", "par", None, None),
        P("grp", "par"),
        P("grp", "par"),
        P("grp", "par"),
        P("grp", None),
    )
    out_specs = P(None, ("par", "grp"))
    body = functools.partial(on_device, mesh.shape["grp"], mesh.shape["par"])
    return jax.shard_map(
        body, mesh=mesh, in_specs=in_specs, out_specs=out_specs, check_vma=False
    )
```

time: 171 us -> 43 us (0.25)
  waiting for transfers between devices: 116 us -> 0 us
  Pallas kernels: 0 us -> 40.3 us
  other arithmetic: 26.1 us -> 0 us
  between operations: 14.2 us -> 0.66 us
  matrix products: 10.7 us -> 0 us
  local copies, waits for them, and re-layouts: 4.02 us -> 1.87 us
    psum x1 -> x0, waiting for transfers between devices: 96 us -> none  [on_device(): fwd = lax.psum(partial_value, 'par')]
    pallas_call x0 -> x1, Pallas kernels: none -> 40.3 us  [on_device(): pl.pallas_call(functools.partial(kernel, n, groups), out_shape=jax.ShapeD...]
    scatter-add x2 -> x0, other arithmetic: 23.4 us -> none  [the longest x1 11.7 us: on_device(): local_terms = jax.ops.segment_sum(back, bparam, num_segments=pblocks)]
    reduce_scatter x1 -> x0, waiting for transfers between devices: 19.7 us -> none  [on_device(): return lax.psum_scatter(local_terms, 'grp', scatter_dimension=1, tiled=True)]
    dot_general x2 -> x0, matrix products: 10.7 us -> none  [the longest x1 5.88 us: on_device(): jnp.einsum('kco,cpo->ckp', pickv, blocks, preferred_element_type=jnp.floa...]
    reshape x3 -> x0, local copies, waits for them, and re-layouts: 2.25 us -> none  [the longest x1 1.1 us: on_device(): jnp.transpose(partial_value, (1, 0, 2)).reshape(probes, oblocks * width)]
    unnamed x8 -> x1, local copies, waits for them, and re-layouts: 0.02 us -> 1.87 us
  transfers between devices with their start and end apart: 2 -> 0, of which waited for: 2 -> 0; matrix products, arithmetic and copies ran while one was open for 0% -> 0% of each run, Pallas kernels for 0% -> 0%
where the time goes in v3:
time: 43 us; the launch traced here: 42.9 us
  Pallas kernels  40.3 us (94%)
  local copies, waits for them, and re-layouts  1.87 us (4%)
  between operations  0.66 us (2%)
    pallas_call x1, Pallas kernels, on_device(): pl.pallas_call(functools.partial(kernel, n, groups), out_shape=jax.ShapeD...  40.3 us
    unnamed x1, local copies, waits for them, and re-layouts  1.87 us

profile of v3, /device:TPU:0, one launch (start us, length us, event | category | flops | bytes accessed | tf_op | source)
XLA Modules:
  0.0 42.9 jit_solution(7065453174463104236)
XLA Ops:
  0.7 40.3 %shard_map.64 = f32[32,4096]{1,0:T(8,128)} custom-call(s32[1,128]{1,0:T(1,128)} %bparam_hbm.1, s32[1,128]{1,0:T(1,128)} %bobs_hbm.1, s32[1,1]{1,0:T(1,128)S(6)} %copy.8.count, bf16[32,8192]{1,0:T(8,128)(2,1)} %omega_hbm.1, bf16[1,128,128,128]{3,2,1,0:T(8,128)(2,1)} %blocks_hbm.1, f32[1,8192]{1,0:T(1,128)} %weight_hbm.1), custom_call_target="tpu_custom_call" | custom-call | flops 268435456 | bytes 4194304 | tf_op jit(solution)/shard_map/pallas_call | solution.py:253
  41.0 1.9 %copy.9 = f32[32,4096]{1,0:T(8,128)} copy(f32[32,4096]{1,0:T(8,128)} %shard_map.64) | data formatting | bytes 1048576

commit v4 on v3

v4 whole, which is shorter than its diff:
```python
import functools

import jax
import jax.numpy as jnp
from jax import lax
from jax.experimental import pallas as pl
from jax.experimental.pallas import tpu as pltpu
from jax.sharding import PartitionSpec as P

MESH = pl.DeviceIdType.MESH
STEP = 16
ROWS = 16
LEVELS = 32000.0
VMEM_LIMIT = 57 * 1024 * 1024


def kernel(
    n, groups,
    bparam_hbm, bobs_hbm, count, omega_hbm, blocks_hbm, weight_hbm, own_ref, xrecv,
    bparam, bobs, bparam_row, bobs_row, omega, panels, weight, blocks,
    terms, part, scaled, sib, sbuf, rbuf, sscale, rscale, zsbuf, zrbuf, zsscale, zrscale,
    half_out, xsend,
    small, big, s1, r1, s2, r2, s3, r3, s4, r4, s5, r5, s6, s7, r7, s8, r8, sx, rx,
):
    me = lax.axis_index("par")
    g = lax.axis_index("grp")
    probes = omega.shape[0]
    slots, width = blocks.shape[0], blocks.shape[1]
    oblocks = weight.shape[1] // width
    pblocks = omega.shape[1] // width
    per = pblocks // groups
    chips = n // 2
    rows = 2
    cols = chips // rows
    q, c = me // 2, lax.rem(me, 2)
    z, y = q // rows, lax.rem(q, rows)
    half = oblocks // 2
    nb = half // chips
    mate = {"par": 2 * q + 1 - c}
    beside = {"par": 2 * (rows * z + 1 - y) + c}

    parts = probes // ROWS

    def zed(i):
        return lax.rem(z + i, cols)

    def at_z(i):
        return {"par": 2 * (rows * zed(i) + y) + c}

    def other(i):
        return lax.rem(g + i, groups)

    def lines(block, length):
        return pl.ds(pl.multiple_of(block * probes, probes), length * probes)

    def part_lines(h, block, length):
        at = (h * oblocks + block) * ROWS
        return pl.ds(pl.multiple_of(at, ROWS), length * ROWS)

    def mine(p):
        return pl.ds(c * half + p * nb, nb)

    def theirs(p):
        return pl.ds((1 - c) * half + p * nb, nb)

    early = [
        pltpu.make_async_copy(bparam_hbm, bparam, small.at[0]),
        pltpu.make_async_copy(bobs_hbm, bobs, small.at[1]),
        pltpu.make_async_copy(omega_hbm, omega, small.at[2]),
        pltpu.make_async_copy(bparam_hbm, bparam_row, small.at[3]),
        pltpu.make_async_copy(bobs_hbm, bobs_row, small.at[4]),
        pltpu.make_async_copy(weight_hbm, weight, small.at[5]),
    ]

    def blocks_of(i):
        at = pl.ds(i * STEP, STEP)
        return pltpu.make_async_copy(blocks_hbm.at[0, at], blocks.at[at], big.at[i])

    for copy in early:
        copy.start()
    for i in range(slots // STEP):
        blocks_of(i).start()

    barrier = pltpu.get_barrier_semaphore()
    pl.semaphore_signal(barrier, inc=1, device_id=mate, device_id_type=MESH)
    pl.semaphore_signal(barrier, inc=1, device_id=beside, device_id_type=MESH)
    for i in range(1, cols):
        pl.semaphore_signal(barrier, inc=1, device_id=at_z(i), device_id_type=MESH)
    for i in range(1, groups):
        pl.semaphore_signal(barrier, inc=1, device_id={"grp": other(i)}, device_id_type=MESH)

    for copy in early:
        copy.wait()
    for b in range(pblocks):
        panels[b] = omega[:, b * width:(b + 1) * width]

    def fwd_step(i, carry):
        blocks_of(i).wait()
        for j in range(STEP):
            s = i * STEP + j
            terms[lines(s, 1)] = jnp.dot(
                panels[bparam[0, s]], blocks[s], preferred_element_type=jnp.float32)
        return carry

    lax.fori_loop(0, slots // STEP, fwd_step, 0)

    used = lax.broadcasted_iota(jnp.int32, (1, slots), 1) < count[0, 0]

    def chooser(row, first, length):
        place = lax.broadcasted_iota(jnp.int32, (length, slots), 0) + first
        chosen = jnp.where((place == row) & used, 1.0, 0.0).astype(jnp.bfloat16)
        return jnp.concatenate([chosen, chosen], axis=1)

    def summed(chosen, k):
        value = terms[pl.ds(k, slots, stride=probes), :]
        high = value.astype(jnp.bfloat16)
        low = (value - high.astype(jnp.float32)).astype(jnp.bfloat16)
        return jnp.dot(
            chosen, jnp.concatenate([high, low], axis=0), preferred_element_type=jnp.float32)

    def remote(src, dst, send, recv, device):
        return pltpu.make_async_remote_copy(
            src_ref=src, dst_ref=dst, send_sem=send, recv_sem=recv,
            device_id=device, device_id_type=MESH)

    row_blocks = cols * nb

    def to_mate(h, r):
        return remote(
            part.at[part_lines(h, (1 - c) * half + r * row_blocks, row_blocks)],
            sib.at[h, r], s1.at[h, r], r1.at[h, r], mate)

    def to_beside(h):
        return remote(sbuf.at[h], rbuf.at[h], s2.at[h], r2.at[h], beside)

    def scale_to_beside(h):
        return remote(sscale.at[h], rscale.at[h], s5.at[h], r5.at[h], beside)

    def to_z(h, i, lands):
        return remote(
            zsbuf.at[h, zed(i)], zrbuf.at[h, lands], s7.at[h, zed(i)], r7.at[h, lands], at_z(i))

    def scale_to_z(h, i, lands):
        return remote(zsscale.at[h], zrscale.at[h, lands], s8.at[h, zed(i)], r8.at[h, lands], at_z(i))

    def gather_z(h, p, i):
        piece = scaled.at[h, mine(p)]
        return remote(piece, piece, s3.at[h, zed(i)], r3.at[h, p], at_z(i))

    def gather_beside(h, p):
        piece = scaled.at[h, mine(p)]
        return remote(piece, piece, s6.at[h, p], r3.at[h, p], beside)

    def hand_over(h, p):
        piece = scaled.at[h, mine(p)]
        return remote(piece, piece, s4.at[h, p], r4.at[h, p], mate)

    def take_over(h, p):
        piece = scaled.at[h, theirs(p)]
        return remote(piece, piece, s4.at[h, p], r4.at[h, p], mate)

    def coded(value):
        largest = jnp.maximum(jnp.max(jnp.abs(value), axis=0, keepdims=True), 1e-30)
        level = jnp.round(value * (LEVELS / largest)).astype(jnp.int32).astype(jnp.int16)
        return level, jnp.broadcast_to(largest * (1.0 / LEVELS), (8, width))

    def decoded(level, scale):
        return level.astype(jnp.int32).astype(jnp.float32) * scale[0:1]

    def row_sum(h, r):
        to_mate(h, r).wait_recv()
        return part[part_lines(h, c * half + r * row_blocks, row_blocks), :] + sib[h, r]

    by_obs = chooser(bobs_row[...], 0, oblocks)
    for h in range(parts):
        for k in range(ROWS):
            part[pl.ds(h * oblocks * ROWS + k, oblocks, stride=ROWS), :] = summed(
                by_obs, h * ROWS + k)
        if h == 0:
            pl.semaphore_wait(barrier, cols + groups)
        to_mate(h, 1 - y).start()
        to_mate(h, y).start()
    for h in range(parts):
        level, scale = coded(row_sum(h, 1 - y))
        sscale[h] = scale
        scale_to_beside(h).start()
        sbuf[h] = level
        to_beside(h).start()
    totals = []
    for h in range(parts):
        value = row_sum(h, y)
        scale_to_beside(h).wait_recv()
        to_beside(h).wait_recv()
        value += decoded(rbuf[h], rscale[h])
        level, scale = coded(value)
        zsscale[h] = scale
        piece = nb * ROWS
        for j in range(cols):
            zsbuf[h, j] = level[j * piece:(j + 1) * piece]
        sib[h, y] = value
        for i in range(1, cols):
            scale_to_z(h, i, z).start()
            to_z(h, i, z).start()
    for h in range(parts):
        at = pl.ds(pl.multiple_of(z * piece, piece), piece)
        total = sib[h, y, at, :]
        for i in range(1, cols):
            scale_to_z(h, i, zed(i)).wait_recv()
            to_z(h, i, zed(i)).wait_recv()
            total += decoded(zrbuf[h, zed(i)], zrscale[h, zed(i)])
        p = y * cols + z
        for b in range(nb):
            block = c * half + p * nb + b
            factor = weight[0:1, pl.ds(pl.multiple_of(block * width, width), width)]
            scaled[h, block] = (total[b * ROWS:(b + 1) * ROWS] * factor).astype(scaled.dtype)
        gather_beside(h, p).start()
        for i in range(1, cols):
            gather_z(h, p, i).start()
        hand_over(h, p).start()
    for h in range(parts):
        for i in range(1, cols):
            p = y * cols + zed(i)
            gather_z(h, p, i).wait_recv()
            gather_beside(h, p).start()
            hand_over(h, p).start()
    for h in range(parts):
        for i in range(cols):
            p = (1 - y) * cols + zed(i)
            gather_beside(h, p).wait_recv()
            hand_over(h, p).start()
    for h in range(parts):
        for p in range(chips):
            take_over(h, p).wait_recv()

    def back_step(i, carry):
        for j in range(STEP):
            s = i * STEP + j
            terms[lines(s, 1)] = lax.dot_general(
                jnp.concatenate([scaled[h, bobs[0, s]] for h in range(parts)], axis=0), blocks[s],
                (((1,), (1,)), ((), ())), preferred_element_type=jnp.float32)
        return carry

    lax.fori_loop(0, slots // STEP, back_step, 0)

    def exchange(i, slot, h):
        at = pl.ds(h * ROWS, ROWS)
        return remote(
            xsend.at[i - 1, at], xrecv.at[slot, at], sx.at[i - 1, h], rx.at[slot, h],
            {"grp": other(i)})

    for i in range(1, groups):
        chosen = chooser(bparam_row[...], other(i) * per, per)
        for h in range(parts):
            for k in range(ROWS):
                half_out[pl.ds(k, per, stride=ROWS), :] = summed(chosen, h * ROWS + k)
            for b in range(per):
                xsend[i - 1, h * ROWS:(h + 1) * ROWS, b * width:(b + 1) * width] = (
                    half_out[b * ROWS:(b + 1) * ROWS, :].astype(xsend.dtype))
            exchange(i, groups - i - 1, h).start()
    chosen = chooser(bparam_row[...], g * per, per)
    for h in range(parts):
        for k in range(ROWS):
            half_out[pl.ds(k, per, stride=ROWS), :] = summed(chosen, h * ROWS + k)
        for b in range(per):
            own_ref[h * ROWS:(h + 1) * ROWS, b * width:(b + 1) * width] = (
                half_out[b * ROWS:(b + 1) * ROWS, :])

    for h in range(parts):
        for r in range(rows):
            to_mate(h, r).wait_send()
        to_beside(h).wait_send()
        scale_to_beside(h).wait_send()
        for i in range(1, cols):
            to_z(h, i, z).wait_send()
            scale_to_z(h, i, z).wait_send()
            gather_z(h, y * cols + z, i).wait_send()
        for i in range(cols):
            gather_beside(h, y * cols + i).wait_send()
        for p in range(chips):
            hand_over(h, p).wait_send()
    for i in range(1, groups):
        for h in range(parts):
            exchange(i, groups - i - 1, h).wait_send()
            exchange(i, i - 1, h).wait_recv()


def on_device(groups, n, omega, blocks, bparam, bobs, count, weights):
    probes = omega.shape[0]
    slots, width = blocks.shape[1], blocks.shape[2]
    oblocks = weights.shape[1] // width
    pblocks = omega.shape[1] // width
    per = pblocks // groups
    chips = n // 2
    cols = chips // 2
    row = cols * (oblocks // n) * ROWS
    piece = oblocks // n * ROWS
    parts = probes // ROWS
    dma = pltpu.SemaphoreType.DMA
    hbm = pl.BlockSpec(memory_space=pl.ANY)
    vmem = pl.BlockSpec(memory_space=pltpu.VMEM)
    own, others = pl.pallas_call(
        functools.partial(kernel, n, groups),
        out_shape=(
            jax.ShapeDtypeStruct((probes, per * width), jnp.float32),
            jax.ShapeDtypeStruct((groups - 1, probes, per * width), jnp.bfloat16),
        ),
        in_specs=[hbm, hbm, pl.BlockSpec(memory_space=pltpu.SMEM), hbm, hbm, hbm],
        out_specs=(vmem, vmem),
        scratch_shapes=[
            pltpu.SMEM(bparam.shape, jnp.int32),
            pltpu.SMEM(bobs.shape, jnp.int32),
            pltpu.VMEM(bparam.shape, jnp.int32),
            pltpu.VMEM(bobs.shape, jnp.int32),
            pltpu.VMEM(omega.shape, omega.dtype),
            pltpu.VMEM((pblocks, probes, width), omega.dtype),
            pltpu.VMEM(weights.shape, weights.dtype),
            pltpu.VMEM(blocks.shape[1:], blocks.dtype),
            pltpu.VMEM((slots * probes, width), jnp.float32),
            pltpu.VMEM((oblocks * probes, width), jnp.float32),
            pltpu.VMEM((parts, oblocks, ROWS, width), jnp.bfloat16),
            pltpu.VMEM((parts, 2, row, width), jnp.float32),
            pltpu.VMEM((parts, row, width), jnp.int16),
            pltpu.VMEM((parts, row, width), jnp.int16),
            pltpu.VMEM((parts, 8, width), jnp.float32),
            pltpu.VMEM((parts, 8, width), jnp.float32),
            pltpu.VMEM((parts, cols, piece, width), jnp.int16),
            pltpu.VMEM((parts, cols, piece, width), jnp.int16),
            pltpu.VMEM((parts, 8, width), jnp.float32),
            pltpu.VMEM((parts, cols, 8, width), jnp.float32),
            pltpu.VMEM((per * ROWS, width), jnp.float32),
            pltpu.VMEM((groups - 1, probes, per * width), jnp.bfloat16),
            dma((6,)),
            dma((slots // STEP,)),
            dma((parts, 2)), dma((parts, 2)),
            dma((parts,)), dma((parts,)),
            dma((parts, cols)), dma((parts, chips)),
            dma((parts, chips)), dma((parts, chips)),
            dma((parts,)), dma((parts,)),
            dma((parts, chips)),
            dma((parts, cols)), dma((parts, cols)),
            dma((parts, cols)), dma((parts, cols)),
            dma((groups - 1, parts)), dma((groups - 1, parts)),
        ],
        compiler_params=pltpu.CompilerParams(
            collective_id=0, has_side_effects=True, vmem_limit_bytes=VMEM_LIMIT),
        cost_estimate=pl.CostEstimate(
            flops=4 * slots * probes * width * width,
            bytes_accessed=2 * slots * width * width, transcendentals=0),
    )(bparam, bobs, count, omega, blocks, weights)
    return own + jnp.sum(others.astype(jnp.float32), axis=0)


def solution(mesh):
    in_specs = (
        P(None, "par"),
        P("grp", "par", None, None),
        P("grp", "par"),
        P("grp", "par"),
        P("grp", "par"),
        P("grp", None),
    )
    out_specs = P(None, ("par", "grp"))
    body = functools.partial(on_device, mesh.shape["grp"], mesh.shape["par"])
    return jax.shard_map(
        body, mesh=mesh, in_specs=in_specs, out_specs=out_specs, check_vma=False
    )
```

time: 43 us -> 41.8 us (0.972)
  other arithmetic: 0 us -> 1.95 us
  local copies, waits for them, and re-layouts: 1.87 us -> 0 us
  Pallas kernels: 40.3 us -> 39.1 us
    add x0 -> x1, other arithmetic: none -> 1.95 us  [on_device(): return own + jnp.sum(others.astype(jnp.float32), axis=0)]
    unnamed x1 -> x0, local copies, waits for them, and re-layouts: 1.87 us -> none
    pallas_call x1, Pallas kernels: 40.3 us -> 39.1 us  [on_device(): pl.pallas_call(functools.partial(kernel, n, groups), out_shape=(jax.Shape...]
where the time goes in v4:
time: 41.8 us; the launch traced here: 41.7 us
  Pallas kernels  39.1 us (94%)
  other arithmetic  1.95 us (5%)
  between operations  0.66 us (2%)
    pallas_call x1, Pallas kernels, on_device(): pl.pallas_call(functools.partial(kernel, n, groups), out_shape=(jax.Shape...  39.1 us
    add x1, other arithmetic, on_device(): return own + jnp.sum(others.astype(jnp.float32), axis=0)  1.95 us

profile of v4, /device:TPU:0, one launch (start us, length us, event | category | flops | bytes accessed | tf_op | source)
XLA Modules:
  0.0 41.7 jit_solution(14862625600512012616)
XLA Ops:
  0.7 39.1 %shard_map.64 = (f32[32,4096]{1,0:T(8,128)}, bf16[1,32,4096]{2,1,0:T(8,128)(2,1)}) custom-call(s32[1,128]{1,0:T(1,128)} %bparam_hbm.1, s32[1,128]{1,0:T(1,128)} %bobs_hbm.1, s32[1,1]{1,0:T(1,128)S(6)} %copy.7.count, bf16[32,8192]{1,0:T(8,128)(2,1)} %omega_hbm.1, bf16[1,128,128,128]{3,2,1,0:T(8,128)(2,1)} %blocks_hbm.1, f32[1,8192]{1,0:T(1,128)} %weight_hbm.1), custom_call_target="tpu_custom_call" | custom-call | flops 268435456 | bytes 4194304 | tf_op jit(solution)/shard_map/pallas_call | solution.py:301
  39.7 1.9 %convert_add_fusion = f32[32,4096]{1,0:T(8,128)} fusion(f32[32,4096]{1,0:T(8,128)} %get-tuple-element.7, bf16[1,32,4096]{2,1,0:T(8,128)(2,1)} %get-tuple-element.8), kind=kLoop, calls=%fused_computation | loop fusion | flops 262144 | bytes 1310720 | tf_op jit(solution)/shard_map/add | solution.py:350

commit v5 on v4

--- a/solution.py
+++ b/solution.py
@@ -10,6 +10,7 @@
 MESH = pl.DeviceIdType.MESH
 STEP = 16
 ROWS = 16
+WIDE = 4
 LEVELS = 32000.0
 VMEM_LIMIT = 57 * 1024 * 1024
 
@@ -18,9 +19,9 @@
     n, groups,
     bparam_hbm, bobs_hbm, count, omega_hbm, blocks_hbm, weight_hbm, own_ref, xrecv,
     bparam, bobs, bparam_row, bobs_row, omega, panels, weight, blocks,
-    terms, part, scaled, sib, sbuf, rbuf, sscale, rscale, zsbuf, zrbuf, zsscale, zrscale,
-    half_out, xsend,
-    small, big, s1, r1, s2, r2, s3, r3, s4, r4, s5, r5, s6, s7, r7, s8, r8, sx, rx,
+    terms, split, part, scaled, sib, sbuf, rbuf, sscale, rscale, zsbuf, zrbuf, zsscale, zrscale,
+    half_out, own, xsend,
+    small, big, s1, r1, s2, r2, s3, r3, s4, r4, s5, r5, s6, s7, r7, s8, r8, sx, rx, so,
 ):
     me = lax.axis_index("par")
     g = lax.axis_index("grp")
@@ -111,12 +112,17 @@
         chosen = jnp.where((place == row) & used, 1.0, 0.0).astype(jnp.bfloat16)
         return jnp.concatenate([chosen, chosen], axis=1)
 
+    def spread(h):
+        for k in range(h * ROWS, (h + 1) * ROWS):
+            value = terms[pl.ds(k, slots, stride=probes), :]
+            high = value.astype(jnp.bfloat16)
+            split[0:slots, k * width:(k + 1) * width] = high
+            split[slots:, k * width:(k + 1) * width] = (
+                value - high.astype(jnp.float32)).astype(jnp.bfloat16)
+
     def summed(chosen, k):
-        value = terms[pl.ds(k, slots, stride=probes), :]
-        high = value.astype(jnp.bfloat16)
-        low = (value - high.astype(jnp.float32)).astype(jnp.bfloat16)
         return jnp.dot(
-            chosen, jnp.concatenate([high, low], axis=0), preferred_element_type=jnp.float32)
+            chosen, split[:, k * width:(k + WIDE) * width], preferred_element_type=jnp.float32)
 
     def remote(src, dst, send, recv, device):
         return pltpu.make_async_remote_copy(
@@ -173,9 +179,12 @@
 
     by_obs = chooser(bobs_row[...], 0, oblocks)
     for h in range(parts):
-        for k in range(ROWS):
-            part[pl.ds(h * oblocks * ROWS + k, oblocks, stride=ROWS), :] = summed(
-                by_obs, h * ROWS + k)
+        spread(h)
+        for k in range(0, ROWS, WIDE):
+            value = summed(by_obs, h * ROWS + k)
+            for j in range(WIDE):
+                part[pl.ds(h * oblocks * ROWS + k + j, oblocks, stride=ROWS), :] = (
+                    value[:, j * width:(j + 1) * width])
         if h == 0:
             pl.semaphore_wait(barrier, cols + groups)
         to_mate(h, 1 - y).start()
@@ -242,28 +251,39 @@
 
     lax.fori_loop(0, slots // STEP, back_step, 0)
 
+    def keep(h):
+        at = pl.ds(h * ROWS, ROWS)
+        return pltpu.make_async_copy(own.at[at], own_ref.at[at], so.at[h])
+
     def exchange(i, slot, h):
         at = pl.ds(h * ROWS, ROWS)
         return remote(
             xsend.at[i - 1, at], xrecv.at[slot, at], sx.at[i - 1, h], rx.at[slot, h],
             {"grp": other(i)})
 
+    def placed(chosen, h):
+        for k in range(0, ROWS, WIDE):
+            value = summed(chosen, h * ROWS + k)
+            for j in range(WIDE):
+                half_out[pl.ds(k + j, per, stride=ROWS), :] = value[:, j * width:(j + 1) * width]
+
     for i in range(1, groups):
         chosen = chooser(bparam_row[...], other(i) * per, per)
         for h in range(parts):
-            for k in range(ROWS):
-                half_out[pl.ds(k, per, stride=ROWS), :] = summed(chosen, h * ROWS + k)
+            if i == 1:
+                spread(h)
+            placed(chosen, h)
             for b in range(per):
                 xsend[i - 1, h * ROWS:(h + 1) * ROWS, b * width:(b + 1) * width] = (
                     half_out[b * ROWS:(b + 1) * ROWS, :].astype(xsend.dtype))
             exchange(i, groups - i - 1, h).start()
     chosen = chooser(bparam_row[...], g * per, per)
     for h in range(parts):
-        for k in range(ROWS):
-            half_out[pl.ds(k, per, stride=ROWS), :] = summed(chosen, h * ROWS + k)
+        placed(chosen, h)
         for b in range(per):
-            own_ref[h * ROWS:(h + 1) * ROWS, b * width:(b + 1) * width] = (
+            own[h * ROWS:(h + 1) * ROWS, b * width:(b + 1) * width] = (
                 half_out[b * ROWS:(b + 1) * ROWS, :])
+        keep(h).start()
 
     for h in range(parts):
         for r in range(rows):
@@ -282,6 +302,8 @@
         for h in range(parts):
             exchange(i, groups - i - 1, h).wait_send()
             exchange(i, i - 1, h).wait_recv()
+    for h in range(parts):
+        keep(h).wait()
 
 
 def on_device(groups, n, omega, blocks, bparam, bobs, count, weights):
@@ -297,7 +319,6 @@
     parts = probes // ROWS
     dma = pltpu.SemaphoreType.DMA
     hbm = pl.BlockSpec(memory_space=pl.ANY)
-    vmem = pl.BlockSpec(memory_space=pltpu.VMEM)
     own, others = pl.pallas_call(
         functools.partial(kernel, n, groups),
         out_shape=(
@@ -305,7 +326,7 @@
             jax.ShapeDtypeStruct((groups - 1, probes, per * width), jnp.bfloat16),
         ),
         in_specs=[hbm, hbm, pl.BlockSpec(memory_space=pltpu.SMEM), hbm, hbm, hbm],
-        out_specs=(vmem, vmem),
+        out_specs=(hbm, hbm),
         scratch_shapes=[
             pltpu.SMEM(bparam.shape, jnp.int32),
             pltpu.SMEM(bobs.shape, jnp.int32),
@@ -316,6 +337,7 @@
             pltpu.VMEM(weights.shape, weights.dtype),
             pltpu.VMEM(blocks.shape[1:], blocks.dtype),
             pltpu.VMEM((slots * probes, width), jnp.float32),
+            pltpu.VMEM((2 * slots, probes * width), jnp.bfloat16),
             pltpu.VMEM((oblocks * probes, width), jnp.float32),
             pltpu.VMEM((parts, oblocks, ROWS, width), jnp.bfloat16),
             pltpu.VMEM((parts, 2, row, width), jnp.float32),
@@ -328,6 +350,7 @@
             pltpu.VMEM((parts, 8, width), jnp.float32),
             pltpu.VMEM((parts, cols, 8, width), jnp.float32),
             pltpu.VMEM((per * ROWS, width), jnp.float32),
+            pltpu.VMEM((probes, per * width), jnp.float32),
             pltpu.VMEM((groups - 1, probes, per * width), jnp.bfloat16),
             dma((6,)),
             dma((slots // STEP,)),
@@ -339,7 +362,7 @@
             dma((parts, chips)),
             dma((parts, cols)), dma((parts, cols)),
             dma((parts, cols)), dma((parts, cols)),
-            dma((groups - 1, parts)), dma((groups - 1, parts)),
+            dma((groups - 1, parts)), dma((groups - 1, parts)), dma((parts,)),
         ],
         compiler_params=pltpu.CompilerParams(
             collective_id=0, has_side_effects=True, vmem_limit_bytes=VMEM_LIMIT),

time: 41.8 us -> 41.5 us (level)
  no operation moved by 1% of the time
where the time goes in v5:
time: 41.5 us; the launch traced here: 41.3 us
  Pallas kernels  38.7 us (93%)
  other arithmetic  1.95 us (5%)
  between operations  0.66 us (2%)
    pallas_call x1, Pallas kernels, on_device(): pl.pallas_call(functools.partial(kernel, n, groups), out_shape=(jax.Shape...  38.7 us
    add x1, other arithmetic, on_device(): return own + jnp.sum(others.astype(jnp.float32), axis=0)  1.95 us

profile of v5, /device:TPU:0, one launch (start us, length us, event | category | flops | bytes accessed | tf_op | source)
XLA Modules:
  0.0 41.3 jit_solution(8327154541606148785)
XLA Ops:
  0.7 38.7 %shard_map.64 = (f32[32,4096]{1,0:T(8,128)}, bf16[1,32,4096]{2,1,0:T(8,128)(2,1)}) custom-call(s32[1,128]{1,0:T(1,128)} %bparam_hbm.1, s32[1,128]{1,0:T(1,128)} %bobs_hbm.1, s32[1,1]{1,0:T(1,128)S(6)} %copy.7.count, bf16[32,8192]{1,0:T(8,128)(2,1)} %omega_hbm.1, bf16[1,128,128,128]{3,2,1,0:T(8,128)(2,1)} %blocks_hbm.1, f32[1,8192]{1,0:T(1,128)} %weight_hbm.1), custom_call_target="tpu_custom_call" | custom-call | flops 268435456 | bytes 4194304 | tf_op jit(solution)/shard_map/pallas_call | solution.py:322
  39.4 1.9 %convert_add_fusion = f32[32,4096]{1,0:T(8,128)} fusion(f32[32,4096]{1,0:T(8,128)} %get-tuple-element.7, bf16[1,32,4096]{2,1,0:T(8,128)(2,1)} %get-tuple-element.8), kind=kLoop, calls=%fused_computation | loop fusion | flops 262144 | bytes 1310720 | tf_op jit(solution)/shard_map/add | solution.py:373

commit v6 on v5

--- a/solution.py
+++ b/solution.py
@@ -10,6 +10,7 @@
 MESH = pl.DeviceIdType.MESH
 STEP = 16
 ROWS = 16
+TAIL = 16
 WIDE = 4
 LEVELS = 32000.0
 VMEM_LIMIT = 57 * 1024 * 1024
@@ -19,9 +20,9 @@
     n, groups,
     bparam_hbm, bobs_hbm, count, omega_hbm, blocks_hbm, weight_hbm, own_ref, xrecv,
     bparam, bobs, bparam_row, bobs_row, omega, panels, weight, blocks,
-    terms, split, part, scaled, sib, sbuf, rbuf, sscale, rscale, zsbuf, zrbuf, zsscale, zrscale,
+    terms, split, part, scaled, sib, sbuf, rbuf, zsbuf, zrbuf,
     half_out, own, xsend,
-    small, big, s1, r1, s2, r2, s3, r3, s4, r4, s5, r5, s6, s7, r7, s8, r8, sx, rx, so,
+    small, big, s1, r1, s2, r2, s3, r3, s4, r4, s6, r6, s7, r7, sx, rx, so,
 ):
     me = lax.axis_index("par")
     g = lax.axis_index("grp")
@@ -61,9 +62,6 @@
     def mine(p):
         return pl.ds(c * half + p * nb, nb)
 
-    def theirs(p):
-        return pl.ds((1 - c) * half + p * nb, nb)
-
     early = [
         pltpu.make_async_copy(bparam_hbm, bparam, small.at[0]),
         pltpu.make_async_copy(bobs_hbm, bobs, small.at[1]),
@@ -139,39 +137,36 @@
     def to_beside(h):
         return remote(sbuf.at[h], rbuf.at[h], s2.at[h], r2.at[h], beside)
 
-    def scale_to_beside(h):
-        return remote(sscale.at[h], rscale.at[h], s5.at[h], r5.at[h], beside)
-
     def to_z(h, i, lands):
         return remote(
             zsbuf.at[h, zed(i)], zrbuf.at[h, lands], s7.at[h, zed(i)], r7.at[h, lands], at_z(i))
 
-    def scale_to_z(h, i, lands):
-        return remote(zsscale.at[h], zrscale.at[h, lands], s8.at[h, zed(i)], r8.at[h, lands], at_z(i))
-
     def gather_z(h, p, i):
         piece = scaled.at[h, mine(p)]
         return remote(piece, piece, s3.at[h, zed(i)], r3.at[h, p], at_z(i))
 
-    def gather_beside(h, p):
-        piece = scaled.at[h, mine(p)]
-        return remote(piece, piece, s6.at[h, p], r3.at[h, p], beside)
-
-    def hand_over(h, p):
-        piece = scaled.at[h, mine(p)]
-        return remote(piece, piece, s4.at[h, p], r4.at[h, p], mate)
-
-    def take_over(h, p):
-        piece = scaled.at[h, theirs(p)]
-        return remote(piece, piece, s4.at[h, p], r4.at[h, p], mate)
+    def row_of(core, r):
+        return pl.ds(core * half + r * row_blocks, row_blocks)
+
+    def gather_beside(h, r):
+        piece = scaled.at[h, row_of(c, r)]
+        return remote(piece, piece, s6.at[h], r6.at[h], beside)
+
+    def hand_over(h, core, r):
+        piece = scaled.at[h, row_of(core, r)]
+        return remote(piece, piece, s4.at[h, r], r4.at[h, r], mate)
 
     def coded(value):
         largest = jnp.maximum(jnp.max(jnp.abs(value), axis=0, keepdims=True), 1e-30)
-        level = jnp.round(value * (LEVELS / largest)).astype(jnp.int32).astype(jnp.int16)
-        return level, jnp.broadcast_to(largest * (1.0 / LEVELS), (8, width))
-
-    def decoded(level, scale):
-        return level.astype(jnp.int32).astype(jnp.float32) * scale[0:1]
+        power = jnp.ceil(jnp.log2(largest))
+        level = jnp.round(value * (jnp.exp2(-power) * LEVELS)).astype(jnp.int32)
+        tail = jnp.broadcast_to(power.astype(jnp.int32), (TAIL, width))
+        return level.astype(jnp.int16), tail.astype(jnp.int16)
+
+    def decoded(message):
+        value = message.astype(jnp.int32).astype(jnp.float32)
+        size = value.shape[0] - TAIL
+        return value[:size] * (jnp.exp2(value[size:size + 1]) * (1.0 / LEVELS))
 
     def row_sum(h, r):
         to_mate(h, r).wait_recv()
@@ -190,56 +185,46 @@
         to_mate(h, 1 - y).start()
         to_mate(h, y).start()
     for h in range(parts):
-        level, scale = coded(row_sum(h, 1 - y))
-        sscale[h] = scale
-        scale_to_beside(h).start()
-        sbuf[h] = level
+        level, tail = coded(row_sum(h, 1 - y))
+        sbuf[h, 0:level.shape[0]] = level
+        sbuf[h, level.shape[0]:] = tail
         to_beside(h).start()
-    totals = []
     for h in range(parts):
         value = row_sum(h, y)
-        scale_to_beside(h).wait_recv()
         to_beside(h).wait_recv()
-        value += decoded(rbuf[h], rscale[h])
-        level, scale = coded(value)
-        zsscale[h] = scale
+        value += decoded(rbuf[h])
+        level, tail = coded(value)
         piece = nb * ROWS
         for j in range(cols):
-            zsbuf[h, j] = level[j * piece:(j + 1) * piece]
+            zsbuf[h, j, 0:piece] = level[j * piece:(j + 1) * piece]
+            zsbuf[h, j, piece:] = tail
         sib[h, y] = value
         for i in range(1, cols):
-            scale_to_z(h, i, z).start()
             to_z(h, i, z).start()
     for h in range(parts):
         at = pl.ds(pl.multiple_of(z * piece, piece), piece)
         total = sib[h, y, at, :]
         for i in range(1, cols):
-            scale_to_z(h, i, zed(i)).wait_recv()
             to_z(h, i, zed(i)).wait_recv()
-            total += decoded(zrbuf[h, zed(i)], zrscale[h, zed(i)])
+            total += decoded(zrbuf[h, zed(i)])
         p = y * cols + z
         for b in range(nb):
             block = c * half + p * nb + b
             factor = weight[0:1, pl.ds(pl.multiple_of(block * width, width), width)]
             scaled[h, block] = (total[b * ROWS:(b + 1) * ROWS] * factor).astype(scaled.dtype)
-        gather_beside(h, p).start()
         for i in range(1, cols):
             gather_z(h, p, i).start()
-        hand_over(h, p).start()
-    for h in range(parts):
-        for i in range(1, cols):
-            p = y * cols + zed(i)
-            gather_z(h, p, i).wait_recv()
-            gather_beside(h, p).start()
-            hand_over(h, p).start()
-    for h in range(parts):
-        for i in range(cols):
-            p = (1 - y) * cols + zed(i)
-            gather_beside(h, p).wait_recv()
-            hand_over(h, p).start()
-    for h in range(parts):
-        for p in range(chips):
-            take_over(h, p).wait_recv()
+    for h in range(parts):
+        for i in range(1, cols):
+            gather_z(h, y * cols + zed(i), i).wait_recv()
+        gather_beside(h, y).start()
+        hand_over(h, c, y).start()
+    for h in range(parts):
+        gather_beside(h, 1 - y).wait_recv()
+        hand_over(h, c, 1 - y).start()
+    for h in range(parts):
+        for r in range(rows):
+            hand_over(h, 1 - c, r).wait_recv()
 
     def back_step(i, carry):
         for j in range(STEP):
@@ -289,15 +274,12 @@
         for r in range(rows):
             to_mate(h, r).wait_send()
         to_beside(h).wait_send()
-        scale_to_beside(h).wait_send()
+        gather_beside(h, y).wait_send()
         for i in range(1, cols):
             to_z(h, i, z).wait_send()
-            scale_to_z(h, i, z).wait_send()
             gather_z(h, y * cols + z, i).wait_send()
-        for i in range(cols):
-            gather_beside(h, y * cols + i).wait_send()
-        for p in range(chips):
-            hand_over(h, p).wait_send()
+        for r in range(rows):
+            hand_over(h, c, r).wait_send()
     for i in range(1, groups):
         for h in range(parts):
             exchange(i, groups - i - 1, h).wait_send()
@@ -341,14 +323,10 @@
             pltpu.VMEM((oblocks * probes, width), jnp.float32),
             pltpu.VMEM((parts, oblocks, ROWS, width), jnp.bfloat16),
             pltpu.VMEM((parts, 2, row, width), jnp.float32),
-            pltpu.VMEM((parts, row, width), jnp.int16),
-            pltpu.VMEM((parts, row, width), jnp.int16),
-            pltpu.VMEM((parts, 8, width), jnp.float32),
-            pltpu.VMEM((parts, 8, width), jnp.float32),
-            pltpu.VMEM((parts, cols, piece, width), jnp.int16),
-            pltpu.VMEM((parts, cols, piece, width), jnp.int16),
-            pltpu.VMEM((parts, 8, width), jnp.float32),
-            pltpu.VMEM((parts, cols, 8, width), jnp.float32),
+            pltpu.VMEM((parts, row + TAIL, width), jnp.int16),
+            pltpu.VMEM((parts, row + TAIL, width), jnp.int16),
+            pltpu.VMEM((parts, cols, piece + TAIL, width), jnp.int16),
+            pltpu.VMEM((parts, cols, piece + TAIL, width), jnp.int16),
             pltpu.VMEM((per * ROWS, width), jnp.float32),
             pltpu.VMEM((probes, per * width), jnp.float32),
             pltpu.VMEM((groups - 1, probes, per * width), jnp.bfloat16),
@@ -357,10 +335,8 @@
             dma((parts, 2)), dma((parts, 2)),
             dma((parts,)), dma((parts,)),
             dma((parts, cols)), dma((parts, chips)),
-            dma((parts, chips)), dma((parts, chips)),
+            dma((parts, 2)), dma((parts, 2)),
             dma((parts,)), dma((parts,)),
-            dma((parts, chips)),
-            dma((parts, cols)), dma((parts, cols)),
             dma((parts, cols)), dma((parts, cols)),
             dma((groups - 1, parts)), dma((groups - 1, parts)), dma((parts,)),
         ],

time: 41.5 us -> 41.2 us (level)
  no operation moved by 1% of the time
where the time goes in v6:
time: 41.2 us; the launch traced here: 41.1 us
  Pallas kernels  38.4 us (93%)
  other arithmetic  1.95 us (5%)
  between operations  0.66 us (2%)
    pallas_call x1, Pallas kernels, on_device(): pl.pallas_call(functools.partial(kernel, n, groups), out_shape=(jax.Shape...  38.4 us
    add x1, other arithmetic, on_device(): return own + jnp.sum(others.astype(jnp.float32), axis=0)  1.95 us

profile of v6, /device:TPU:0, one launch (start us, length us, event | category | flops | bytes accessed | tf_op | source)
XLA Modules:
  0.0 41.1 jit_solution(12346814238842359967)
XLA Ops:
  0.7 38.4 %shard_map.64 = (f32[32,4096]{1,0:T(8,128)}, bf16[1,32,4096]{2,1,0:T(8,128)(2,1)}) custom-call(s32[1,128]{1,0:T(1,128)} %bparam_hbm.1, s32[1,128]{1,0:T(1,128)} %bobs_hbm.1, s32[1,1]{1,0:T(1,128)S(6)} %copy.7.count, bf16[32,8192]{1,0:T(8,128)(2,1)} %omega_hbm.1, bf16[1,128,128,128]{3,2,1,0:T(8,128)(2,1)} %blocks_hbm.1, f32[1,8192]{1,0:T(1,128)} %weight_hbm.1), custom_call_target="tpu_custom_call" | custom-call | flops 268435456 | bytes 4194304 | tf_op jit(solution)/shard_map/pallas_call | solution.py:304
  39.1 1.9 %convert_add_fusion = f32[32,4096]{1,0:T(8,128)} fusion(f32[32,4096]{1,0:T(8,128)} %get-tuple-element.7, bf16[1,32,4096]{2,1,0:T(8,128)(2,1)} %get-tuple-element.8), kind=kLoop, calls=%fused_computation | loop fusion | flops 262144 | bytes 1310720 | tf_op jit(solution)/shard_map/add | solution.py:349

commit v7 on v6

--- a/solution.py
+++ b/solution.py
@@ -20,7 +20,7 @@
     n, groups,
     bparam_hbm, bobs_hbm, count, omega_hbm, blocks_hbm, weight_hbm, own_ref, xrecv,
     bparam, bobs, bparam_row, bobs_row, omega, panels, weight, blocks,
-    terms, split, part, scaled, sib, sbuf, rbuf, zsbuf, zrbuf,
+    terms, split, part, scaled, sib, msend, held, sbuf, rbuf, zsbuf, zrbuf,
     half_out, own, xsend,
     small, big, s1, r1, s2, r2, s3, r3, s4, r4, s6, r6, s7, r7, sx, rx, so,
 ):
@@ -131,8 +131,7 @@
 
     def to_mate(h, r):
         return remote(
-            part.at[part_lines(h, (1 - c) * half + r * row_blocks, row_blocks)],
-            sib.at[h, r], s1.at[h, r], r1.at[h, r], mate)
+            msend.at[h, r], sib.at[h, r], s1.at[h, r], r1.at[h, r], mate)
 
     def to_beside(h):
         return remote(sbuf.at[h], rbuf.at[h], s2.at[h], r2.at[h], beside)
@@ -170,7 +169,7 @@
 
     def row_sum(h, r):
         to_mate(h, r).wait_recv()
-        return part[part_lines(h, c * half + r * row_blocks, row_blocks), :] + sib[h, r]
+        return part[part_lines(h, c * half + r * row_blocks, row_blocks), :] + decoded(sib[h, r])
 
     by_obs = chooser(bobs_row[...], 0, oblocks)
     for h in range(parts):
@@ -182,8 +181,11 @@
                     value[:, j * width:(j + 1) * width])
         if h == 0:
             pl.semaphore_wait(barrier, cols + groups)
-        to_mate(h, 1 - y).start()
-        to_mate(h, y).start()
+        for r in (1 - y, y):
+            level, tail = coded(part[part_lines(h, (1 - c) * half + r * row_blocks, row_blocks), :])
+            msend[h, r, 0:level.shape[0]] = level
+            msend[h, r, level.shape[0]:] = tail
+            to_mate(h, r).start()
     for h in range(parts):
         level, tail = coded(row_sum(h, 1 - y))
         sbuf[h, 0:level.shape[0]] = level
@@ -198,12 +200,12 @@
         for j in range(cols):
             zsbuf[h, j, 0:piece] = level[j * piece:(j + 1) * piece]
             zsbuf[h, j, piece:] = tail
-        sib[h, y] = value
+        held[h] = value
         for i in range(1, cols):
             to_z(h, i, z).start()
     for h in range(parts):
         at = pl.ds(pl.multiple_of(z * piece, piece), piece)
-        total = sib[h, y, at, :]
+        total = held[h, at, :]
         for i in range(1, cols):
             to_z(h, i, zed(i)).wait_recv()
             total += decoded(zrbuf[h, zed(i)])
@@ -322,7 +324,9 @@
             pltpu.VMEM((2 * slots, probes * width), jnp.bfloat16),
             pltpu.VMEM((oblocks * probes, width), jnp.float32),
             pltpu.VMEM((parts, oblocks, ROWS, width), jnp.bfloat16),
-            pltpu.VMEM((parts, 2, row, width), jnp.float32),
+            pltpu.VMEM((parts, 2, row + TAIL, width), jnp.int16),
+            pltpu.VMEM((parts, 2, row + TAIL, width), jnp.int16),
+            pltpu.VMEM((parts, row, width), jnp.float32),
             pltpu.VMEM((parts, row + TAIL, width), jnp.int16),
             pltpu.VMEM((parts, row + TAIL, width), jnp.int16),
             pltpu.VMEM((parts, cols, piece + TAIL, width), jnp.int16),

time: 41.2 us -> 41.3 us (level)
  no operation moved by 1% of the time
where the time goes in v7:
time: 41.3 us; the launch traced here: 41.2 us
  Pallas kernels  38.5 us (93%)
  other arithmetic  1.95 us (5%)
  between operations  0.66 us (2%)
    pallas_call x1, Pallas kernels, on_device(): pl.pallas_call(functools.partial(kernel, n, groups), out_shape=(jax.Shape...  38.5 us
    add x1, other arithmetic, on_device(): return own + jnp.sum(others.astype(jnp.float32), axis=0)  1.95 us

profile of v7, /device:TPU:0, one launch (start us, length us, event | category | flops | bytes accessed | tf_op | source)
XLA Modules:
  0.0 41.2 jit_solution(15499410336516306022)
XLA Ops:
  0.7 38.5 %shard_map.64 = (f32[32,4096]{1,0:T(8,128)}, bf16[1,32,4096]{2,1,0:T(8,128)(2,1)}) custom-call(s32[1,128]{1,0:T(1,128)} %bparam_hbm.1, s32[1,128]{1,0:T(1,128)} %bobs_hbm.1, s32[1,1]{1,0:T(1,128)S(6)} %copy.7.count, bf16[32,8192]{1,0:T(8,128)(2,1)} %omega_hbm.1, bf16[1,128,128,128]{3,2,1,0:T(8,128)(2,1)} %blocks_hbm.1, f32[1,8192]{1,0:T(1,128)} %weight_hbm.1), custom_call_target="tpu_custom_call" | custom-call | flops 268435456 | bytes 4194304 | tf_op jit(solution)/shard_map/pallas_call | solution.py:306
  39.2 1.9 %convert_add_fusion = f32[32,4096]{1,0:T(8,128)} fusion(f32[32,4096]{1,0:T(8,128)} %get-tuple-element.7, bf16[1,32,4096]{2,1,0:T(8,128)(2,1)} %get-tuple-element.8), kind=kLoop, calls=%fused_computation | loop fusion | flops 262144 | bytes 1310720 | tf_op jit(solution)/shard_map/add | solution.py:353
